TPU v7x, 32 devices: a whole 2x2x4 slice. The times are simulated.
32 devices in a mesh: vocab: 8 (over z, x), rows: 4 (over y, core).
Axes of the slice: x: 2, y: 2, z: 4, core: 2. Of those that a mesh axis runs over, the one named last changes fastest.
Arguments:
- hidden: bfloat16 [1024, 4608], P('rows'), may hold values from -6 to 6
- norm_gain: bfloat16 [4608], replicated, may hold values from 0.5 to 1.5
- embed_table: bfloat16 [16384, 4608], P('vocab', 'rows'), may hold values from -1 to 1
- tokens: int32 [1024], P('rows'), may hold values from 0 to 16383
- parents: int32 [1024], P('rows'), may hold values from 0 to 7
- prev_scores: float32 [1024], P('rows'), may hold values from -30 to -1
- lengths: int32 [1024], P('rows'), may hold values from 1 to 128
Outputs:
- log_probs: float32 [1024, 16384], P('rows', 'vocab')
- chosen_lp: float32 [1024], P('rows')
- normalized: float32 [1024], P('rows')
- next_embed: bfloat16 [1024, 4608], P('rows')
All inputs are finite; a program needn't handle non-finite values.
Results may differ from a plain program's by a relative error of at most 0.0045.
Values may be sent and summed in bfloat16 or wider, within the bound.
A program may use at most 128 MiB of HBM per device.

v0:
```python
import math

import jax
import jax.numpy as jnp
from jax import lax
from jax.sharding import PartitionSpec as P

BEAMS = 8


soft_cap = 30.0
length_power = 0.6
norm_eps = 1e-06


def spread(partial_value, scale):
    terms = partial_value.astype(jnp.float32)
    total = lax.psum(terms, "vocab")
    return (total * scale).astype(jnp.bfloat16)


def local(hidden, norm_gain, embed_table, tokens, parents, prev_scores, lengths):
    shard_index = lax.axis_index("vocab")
    voc_rows = embed_table.shape[0]
    row_count = hidden.shape[0]
    width = hidden.shape[1]
    scale = math.sqrt(width)
    states = hidden.astype(jnp.float32)
    meansq = jnp.mean(states * states, axis=-1, keepdims=True)
    normed = (states * lax.rsqrt(meansq + norm_eps) * norm_gain.astype(jnp.float32)).astype(
        jnp.bfloat16
    )
    local_col = tokens - shard_index * voc_rows
    inside = (local_col >= 0) & (local_col < voc_rows)
    clipped_col = jnp.clip(local_col, 0, voc_rows - 1)
    zero_half = jnp.zeros((), jnp.bfloat16)
    all_tokens = lax.all_gather(tokens, "rows", axis=0, tiled=True)
    feature_cols = lax.all_to_all(normed, "rows", split_axis=1, concat_axis=0, tiled=True)
    logits = lax.psum_scatter(
        lax.dot_general(
            feature_cols, embed_table, (((1,), (1,)), ((), ())), preferred_element_type=jnp.float32
        ).astype(jnp.bfloat16),
        "rows",
        scatter_dimension=0,
        tiled=True,
    ).astype(jnp.float32)
    all_col = all_tokens - shard_index * voc_rows
    all_inside = (all_col >= 0) & (all_col < voc_rows)
    picked = jnp.take(embed_table, jnp.clip(all_col, 0, voc_rows - 1), axis=0)
    picked = jnp.where(all_inside[:, None], picked, zero_half)
    quarters = spread(picked, scale)
    next_embed = lax.all_to_all(quarters, "rows", split_axis=0, concat_axis=1, tiled=True)
    capped = soft_cap * jnp.tanh(logits / soft_cap)
    sum_exp = jnp.sum(jnp.exp(capped), axis=1)
    parent_rows = jnp.arange(row_count, dtype=jnp.int32) // BEAMS * BEAMS + parents
    chosen_local = jnp.where(inside, capped[parent_rows, clipped_col], 0.0)
    total_exp, chosen_logit = lax.psum((sum_exp, chosen_local), "vocab")
    lse = jnp.log(total_exp)
    log_probs = capped - lse[:, None]
    chosen_lp = chosen_logit - lse[parent_rows]
    penalty = jnp.power((5.0 + lengths.astype(jnp.float32)) / 6.0, length_power)
    normalized = (prev_scores[parent_rows] + chosen_lp) / penalty
    return (log_probs, chosen_lp, normalized, next_embed)


def solution(mesh):
    placed = (P("rows", None), P(), P("vocab", "rows"), P("rows"), P("rows"), P("rows"), P("rows"))
    return jax.shard_map(
        local,
        mesh=mesh,
        in_specs=placed,
        out_specs=(P("rows", "vocab"), P("rows"), P("rows"), P("rows", None)),
        check_vma=False,
    )
```

profile of v0, /device:TPU:8, one launch (start us, length us, event | category | flops | bytes accessed | tf_op | source)
XLA Modules:
  0.0 266.3 jit_solution(2609522810245803311)
XLA Ops:
  8.0 0.0 copy-start
  8.0 0.0 all-reduce.3.cloned.1.call-start
  8.1 5.3 %all-gather = s32[4,1,256]{2,1,0:T(1,128)S(1)} all-gather(s32[1,1,256]{2,1,0:T(1,128)} %bitcast.18), channel_id=1, replica_groups=mesh['vocab'=8,'rows'=4] {'rows'}, dimensions={0}, use_global_device_ids=true | all-gather | bytes 5120 | tf_op jit(solution)/shard_map/all_gather | solution.py:37
  13.4 8.5 %gather_fusion.3 = bf16[1024,1152]{1,0:T(8,128)(2,1)S(1)} fusion(bf16[2048,1152]{1,0:T(8,128)(2,1)} %param.9, s32[1024]{0:T(1024)S(1)} %fusion.3), kind=kCustom, calls=%fused_computation.3 | custom fusion | bytes 4722688 | tf_op jit(solution)/shard_map/jit(_take)/gather | solution.py:49
  21.9 2.7 %select_convert_fusion = f32[1024,1152]{1,0:T(8,128)} fusion(bf16[1024,1152]{1,0:T(8,128)(2,1)S(1)} %gather_fusion.3, pred[1024]{0:T(1024)(128)(4,1)S(1)} %compare_and_fusion, pred[1024]{0:T(1024)(128)(4,1)S(1)} %reshape.86), kind=kLoop, calls=%fused_computation.11 | loop fusion | flops 3538944 | bytes 7079936 | tf_op jit(solution)/shard_map/convert_element_type | solution.py:17
  24.6 0.0 copy-start.2
  24.6 0.0 all-reduce.3.cloned.1.call-update
  24.7 0.0 reduce-scatter.2.cloned.1.call-start
  24.7 0.6 copy-done.2
  25.4 2.8 %copy.16 = bf16[256,4608]{0,1:T(8,128)(2,1)S(1)} copy(bf16[256,4608]{1,0:T(8,128)(2,1)} %param.7) | data formatting | bytes 4718592 | tf_op args[0]
  28.2 0.6 fusion
  28.8 2.0 fusion.2
  30.8 31.1 %all_to_all.38 = bf16[256,4,1152]{0,2,1:T(8,128)(2,1)S(1)} all-to-all(bf16[256,4,1152]{0,2,1:T(8,128)(2,1)S(1)} %bitcast.12), channel_id=1, replica_groups=mesh['vocab'=8,'rows'=4] {'rows'}, dimensions={1} | all-to-all | bytes 4718592 | tf_op jit(solution)/shard_map/all_to_all | solution.py:38
  61.9 2.4 copy.17
  64.4 9.6 %convolution_convert_fusion = bf16[1024,2048]{1,0:T(8,128)(2,1)} fusion(bf16[1024,1152]{1,0:T(8,128)(2,1)} %bitcast.15, bf16[2048,1152]{1,0:T(8,128)(2,1)} %param.9), kind=kOutput, calls=%fused_computation.10 | convolution fusion | flops 4833935360 | bytes 11272192 | tf_op jit(solution)/shard_map/dot_general | solution.py:40
  74.0 0.0 reduce-scatter.2.cloned.1.call-update
  74.0 119.7 %all-reduce.3.cloned.1.call-done = f32[1024,1152]{1,0:T(8,128)} async-done(((f32[1024,1152]{1,0:T(8,128)}), f32[1024,1152]{1,0:T(8,128)}) %all-reduce.3.cloned.1.call-update) | async-done | bytes 4718608 | tf_op jit(solution)/shard_map/psum | solution.py:18
  193.7 4.2 %multiply_convert_fusion = bf16[1024,1152]{1,0:T(8,128)(2,1)} fusion(f32[1024,1152]{1,0:T(8,128)} %all-reduce.3.cloned.1.call-done), kind=kLoop, calls=%fused_computation.9 | loop fusion | flops 2359296 | bytes 7077888 | tf_op jit(solution)/shard_map/convert_element_type | solution.py:19
  197.9 0.0 copy-start.3
  197.9 0.0 copy-start.4
  197.9 3.8 %all-to-all-start.1 = ((bf16[4,256,1152]{2,1,0:T(8,128)(2,1)}), bf16[4,256,1152]{2,1,0:T(8,128)(2,1)S(1)}, u32[]{:S(2)}, u32[]{:S(2)}) async-start(bf16[4,256,1152]{2,1,0:T(8,128)(2,1)} %bitcast.5), calls=%async_computation.2 | async-start | bytes 4718592 | tf_op jit(solution)/shard_map/all_to_all | solution.py:52
  201.6 0.0 copy-done.3
  201.6 0.0 copy-done.4
  201.7 0.0 copy-done
  201.7 1.9 gather_fusion.2
  203.7 26.5 %all-to-all-done.1 = bf16[4,256,1152]{2,1,0:T(8,128)(2,1)S(1)} async-done(((bf16[4,256,1152]{2,1,0:T(8,128)(2,1)}), bf16[4,256,1152]{2,1,0:T(8,128)(2,1)S(1)}, u32[]{:S(2)}, u32[]{:S(2)}) %all-to-all-start.1) | async-done | bytes 2359328 | tf_op jit(solution)/shard_map/all_to_all | solution.py:52
  230.1 1.6 copy.19
  231.7 0.0 copy-start.5
  231.7 0.0 reduce-scatter.2.cloned.1.call-done
  231.7 0.0 copy-start.1
  231.7 1.9 tanh_multiply_fusion
  233.7 2.3 gather_fusion
  236.0 18.6 %all-reduce = (f32[256]{0:T(256)S(1)}, f32[256]{0:T(256)S(1)}) all-reduce(f32[256]{0:T(256)S(1)} %get-tuple-element.11, f32[256]{0:T(256)S(1)} %and_select_fusion.1), channel_id=1, replica_groups=mesh['vocab'=8,'rows'=4] {'vocab'}, use_global_device_ids=true, to_apply=%region_3.4 | all-reduce | flops 512 | bytes 4096 | tf_op jit(solution)/shard_map/psum | solution.py:57
  254.6 2.0 gather_fusion.1
  256.6 0.0 copy-done.5
  256.6 0.6 power_multiply_fusion
  257.2 0.0 copy-done.1
  257.2 1.7 broadcast_subtract_fusion
  (11 shorter events, 0.1 us)
Async XLA Ops:
  8.0 193.7 %copy-start = (f32[256]{0:T(256)S(1)}, f32[256]{0:T(256)}, u32[]{:S(2)}) copy-start(f32[256]{0:T(256)} %param.12) | copy-start | bytes 3076
  8.0 185.7 %all-reduce.3.cloned.1.call-start = ((), (), s32[]{:S(2)}) async-start(), calls=%async_computation.4 | async-start | bytes 9437184 | tf_op jit(solution)/shard_map/psum | solution.py:18
  24.6 0.7 copy-start.2
  24.7 207.0 %reduce-scatter.2.cloned.1.call-start = ((), (), s32[]{:S(2)}) async-start(), calls=%async_computation.3 | async-start | bytes 5242880 | tf_op jit(solution)/shard_map/reduce_scatter | solution.py:39
  197.9 3.8 %copy-start.3 = (s32[256]{0:T(256)S(1)}, s32[256]{0:T(256)}, u32[]{:S(2)}) copy-start(s32[256]{0:T(256)} %param.10) | copy-start | bytes 3076
  197.9 3.8 %copy-start.4 = (s32[256]{0:T(256)S(1)}, s32[256]{0:T(256)}, u32[]{:S(2)}) copy-start(s32[256]{0:T(256)} %param.11) | copy-start | bytes 3076
  197.9 32.2 %all-to-all-start.1 = ((bf16[4,256,1152]{2,1,0:T(8,128)(2,1)}), bf16[4,256,1152]{2,1,0:T(8,128)(2,1)S(1)}, u32[]{:S(2)}, u32[]{:S(2)}) async-start(bf16[4,256,1152]{2,1,0:T(8,128)(2,1)} %bitcast.5), calls=%async_computation.2 | async-start | bytes 4718592 | tf_op jit(solution)/shard_map/all_to_all | solution.py:52
  231.7 24.9 %copy-start.5 = (s32[256]{0:T(256)S(1)}, s32[256]{0:T(256)}, u32[]{:S(2)}) copy-start(s32[256]{0:T(256)} %param.13) | copy-start | bytes 3076
  231.7 25.5 %copy-start.1 = (bf16[256,2048]{1,0:T(8,128)(2,1)S(1)}, bf16[256,2048]{1,0:T(8,128)(2,1)}, u32[]{:S(2)}) copy-start(bf16[256,2048]{1,0:T(8,128)(2,1)} %reduce-scatter.2.cloned.1.call-done) | copy-start | bytes 3145732
Sparse Core Ops, SparseCore 0:
  24.8 168.8 all-reduce.2
Sparse Core Ops, SparseCore 1:
  74.1 44.6 reduce-scatter.1
where the time goes:
time: 271 us; the launch traced here: 266 us
  waiting for transfers between devices  146 us (54%)
  blocking collectives  55 us (20%)
  local copies, waits for them, and re-layouts  22.2 us (8%)
  between operations  15.6 us (6%)
  other arithmetic  13.8 us (5%)
  matrix products  9.61 us (4%)
  starting transfers between devices  3.84 us (1%)
    psum x1, waiting for transfers between devices, spread(): total = lax.psum(terms, 'vocab')  120 us
    all_to_all x1, blocking collectives, local(): lax.all_to_all(normed, 'rows', split_axis=1, concat_axis=0, tiled=True)  31.1 us
    all_to_all x1, waiting for transfers between devices, local(): lax.all_to_all(quarters, 'rows', split_axis=0, concat_axis=1, tiled=True)  26.5 us
    psum x1, blocking collectives, local(): total_exp, chosen_logit = lax.psum((sum_exp, chosen_local), 'vocab')  18.6 us
    dot_general x1, matrix products, local(): lax.dot_general(feature_cols, embed_table, (((1,), (1,)), ((), ())), pref...  9.61 us
    gather x1, local copies, waits for them, and re-layouts, local(): picked = jnp.take(embed_table, jnp.clip(all_col, 0, voc_rows - 1), axis=0)  8.46 us
  transfers between devices with their start and end apart: 3, of which 2 were waited for; matrix products, arithmetic and copies ran while one was open for 9% of the time, Pallas kernels for 0%

commit v1 on v0

v1 whole, which is shorter than its diff:
```python
import math

import jax
import jax.numpy as jnp
from jax import lax
from jax.sharding import PartitionSpec as P

BEAMS = 8


soft_cap = 30.0
length_power = 0.6
norm_eps = 1e-06


def by_parent(values, parents):
    groups = values.reshape(-1, 1, BEAMS)
    hit = parents.reshape(-1, BEAMS, 1) == jnp.arange(BEAMS, dtype=jnp.int32)
    return jnp.sum(jnp.where(hit, groups, 0.0), axis=2).reshape(-1)


def local(shards, hidden, norm_gain, embed_table, tokens, parents, prev_scores, lengths):
    shard_index = lax.axis_index("vocab")
    voc_rows = embed_table.shape[0]
    row_count, width = hidden.shape
    scale = math.sqrt(width)

    all_tokens = lax.all_gather(tokens, "rows", axis=0, tiled=False)
    groups = all_tokens.shape[0]
    piece = row_count // shards
    order = all_tokens.reshape(groups, shards, piece).transpose(1, 0, 2).reshape(-1)
    all_col = order - shard_index * voc_rows
    all_inside = (all_col >= 0) & (all_col < voc_rows)
    picked = jnp.take(embed_table, jnp.clip(all_col, 0, voc_rows - 1), axis=0)
    picked = jnp.where(all_inside[:, None], picked, jnp.zeros((), jnp.bfloat16))
    summed = lax.psum_scatter(picked, "vocab", scatter_dimension=0, tiled=True)

    states = hidden.astype(jnp.float32)
    meansq = jnp.mean(states * states, axis=-1, keepdims=True)
    normed = (states * lax.rsqrt(meansq + norm_eps) * norm_gain.astype(jnp.float32)).astype(
        jnp.bfloat16
    )
    feature_cols = lax.all_to_all(normed, "rows", split_axis=1, concat_axis=0, tiled=True)
    logits = lax.psum_scatter(
        lax.dot_general(
            feature_cols, embed_table, (((1,), (1,)), ((), ())), preferred_element_type=jnp.float32
        ).astype(jnp.bfloat16),
        "rows",
        scatter_dimension=0,
        tiled=True,
    ).astype(jnp.float32)

    quarter = lax.all_to_all(summed, "rows", split_axis=0, concat_axis=1, tiled=True)
    quarter = (quarter.astype(jnp.float32) * scale).astype(jnp.bfloat16)
    next_embed = lax.all_gather(quarter, "vocab", axis=0, tiled=True)

    local_col = tokens - shard_index * voc_rows
    inside = (local_col >= 0) & (local_col < voc_rows)
    clipped_col = jnp.clip(local_col, 0, voc_rows - 1)
    capped = soft_cap * jnp.tanh(logits / soft_cap)
    sum_exp = jnp.sum(jnp.exp(capped), axis=1)
    parent_rows = jnp.arange(row_count, dtype=jnp.int32) // BEAMS * BEAMS + parents
    chosen_local = jnp.where(inside, capped[parent_rows, clipped_col], 0.0)
    total_exp, chosen_logit = lax.psum((sum_exp, chosen_local), "vocab")
    lse = jnp.log(total_exp)
    log_probs = capped - lse[:, None]
    chosen_lp = chosen_logit - by_parent(lse, parents)
    penalty = jnp.power((5.0 + lengths.astype(jnp.float32)) / 6.0, length_power)
    normalized = (by_parent(prev_scores, parents) + chosen_lp) / penalty
    return (log_probs, chosen_lp, normalized, next_embed)


def solution(mesh):
    placed = (P("rows", None), P(), P("vocab", "rows"), P("rows"), P("rows"), P("rows"), P("rows"))
    shards = mesh.shape["vocab"]
    return jax.shard_map(
        lambda *args: local(shards, *args),
        mesh=mesh,
        in_specs=placed,
        out_specs=(P("rows", "vocab"), P("rows"), P("rows"), P("rows", None)),
        check_vma=False,
    )
```

time: 271 us -> 233 us (0.86)
  the two profiles are of different devices: /device:TPU:8 before, /device:TPU:0 now
where the time goes in v1:
time: 233 us; the launch traced here: 232 us
  waiting for transfers between devices  115 us (49%)
  blocking collectives  58.7 us (25%)
  local copies, waits for them, and re-layouts  20.1 us (9%)
  between operations  15.7 us (7%)
  matrix products  9.55 us (4%)
  other arithmetic  9.07 us (4%)
  starting transfers between devices  3.57 us (2%)
    reduce_scatter x1, waiting for transfers between devices, local(): summed = lax.psum_scatter(picked, 'vocab', scatter_dimension=0, tiled=True)  68.1 us
    reduce_scatter x1, waiting for transfers between devices, local(): lax.psum_scatter(lax.dot_general(feature_cols, embed_table, (((1,), (1,))...  37.6 us
    all_to_all x1, blocking collectives, local(): lax.all_to_all(normed, 'rows', split_axis=1, concat_axis=0, tiled=True)  31 us
    psum x1, blocking collectives, local(): total_exp, chosen_logit = lax.psum((sum_exp, chosen_local), 'vocab')  21.5 us
    dot_general x1, matrix products, local(): lax.dot_general(feature_cols, embed_table, (((1,), (1,)), ((), ())), pref...  9.55 us
    gather x1, local copies, waits for them, and re-layouts, local(): picked = jnp.take(embed_table, jnp.clip(all_col, 0, voc_rows - 1), axis=0)  8.46 us
    all_gather x1, blocking collectives, local(): all_tokens = lax.all_gather(tokens, 'rows', axis=0, tiled=False)  6.28 us
    all_to_all x1, waiting for transfers between devices, local(): lax.all_to_all(summed, 'rows', split_axis=0, concat_axis=1, tiled=True)  5.66 us
  transfers between devices with their start and end apart: 4, of which 4 were waited for; matrix products, arithmetic and copies ran while one was open for 8% of the time, Pallas kernels for 0%

profile of v1, /device:TPU:0, one launch (start us, length us, event | category | flops | bytes accessed | tf_op | source)
XLA Modules:
  0.0 232.2 jit_solution(5665658368031822061)
XLA Ops:
  8.0 0.0 reduce-scatter.5.cloned.1.call-start
  8.0 6.3 %all-gather.1 = s32[4,1,256]{2,1,0:T(1,128)S(1)} all-gather(s32[1,1,256]{2,1,0:T(1,128)} %bitcast.22), channel_id=2, replica_groups=mesh['vocab'=8,'rows'=4] {'rows'}, dimensions={0}, use_global_device_ids=true | all-gather | bytes 5120 | tf_op jit(solution)/shard_map/all_gather | solution.py:28
  14.4 0.1 min.30
  14.4 0.1 min.34
  14.5 0.1 min.32
  14.7 0.1 reshape.108
  14.8 0.1 and.33
  14.9 8.5 %gather_fusion.1 = bf16[1024,1152]{1,0:T(8,128)(2,1)S(1)} fusion(bf16[2048,1152]{1,0:T(8,128)(2,1)} %param.9, s32[1024]{0:T(1024)S(1)} %broadcast_clamp_fusion), kind=kCustom, calls=%fused_computation.1 | custom fusion | bytes 4722688 | tf_op jit(solution)/shard_map/jit(_take)/gather | solution.py:34
  23.3 2.0 select_select_fusion
  25.4 0.0 reduce-scatter.5.cloned.1.call-update
  25.4 2.8 %copy.26 = bf16[256,4608]{0,1:T(8,128)(2,1)S(1)} copy(bf16[256,4608]{1,0:T(8,128)(2,1)} %param.7) | data formatting | bytes 4718592 | tf_op args[0]
  28.2 0.0 copy-start.2
  28.2 68.1 %reduce-scatter.5.cloned.1.call-done = bf16[128,1152]{1,0:T(8,128)(2,1)} async-done(((bf16[1024,1152]{1,0:T(8,128)(2,1)}), bf16[128,1152]{1,0:T(8,128)(2,1)}) %reduce-scatter.5.cloned.1.call-update) | async-done | bytes 294928 | tf_op jit(solution)/shard_map/reduce_scatter | solution.py:36
  96.3 3.5 %all-to-all-start.1 = ((bf16[4,32,1152]{2,1,0:T(8,128)(2,1)}), bf16[4,32,1152]{2,1,0:T(8,128)(2,1)S(1)}, u32[]{:S(2)}, u32[]{:S(2)}) async-start(bf16[4,32,1152]{2,1,0:T(8,128)(2,1)} %bitcast.18), calls=%async_computation.3 | async-start | bytes 589824 | tf_op jit(solution)/shard_map/all_to_all | solution.py:53
  99.8 0.0 all-gather.4.cloned.1.call-start
  99.8 0.6 fusion
  100.5 5.7 %all-to-all-done.1 = bf16[4,32,1152]{2,1,0:T(8,128)(2,1)S(1)} async-done(((bf16[4,32,1152]{2,1,0:T(8,128)(2,1)}), bf16[4,32,1152]{2,1,0:T(8,128)(2,1)S(1)}, u32[]{:S(2)}, u32[]{:S(2)}) %all-to-all-start.1) | async-done | bytes 294944 | tf_op jit(solution)/shard_map/all_to_all | solution.py:53
  106.1 0.1 fusion.3
  106.2 0.7 copy.37
  106.9 0.0 all-gather.4.cloned.1.call-update
  106.9 0.0 reduce-scatter.3.cloned.1.call-start
  107.0 0.0 copy-done.2
  107.0 2.0 fusion.2
  109.0 31.0 %all_to_all.32 = bf16[256,4,1152]{0,2,1:T(8,128)(2,1)S(1)} all-to-all(bf16[256,4,1152]{0,2,1:T(8,128)(2,1)S(1)} %bitcast.14), channel_id=1, replica_groups=mesh['vocab'=8,'rows'=4] {'rows'}, dimensions={1} | all-to-all | bytes 4718592 | tf_op jit(solution)/shard_map/all_to_all | solution.py:43
  140.0 2.4 %copy.27 = bf16[4,256,1152]{2,1,0:T(8,128)(2,1)} copy(bf16[4,256,1152]{1,2,0:T(8,128)(2,1)S(1)} %bitcast.15) | data formatting | bytes 4718592 | tf_op jit(solution)/shard_map/all_to_all | solution.py:43
  142.4 9.5 %convolution_convert_fusion = bf16[1024,2048]{1,0:T(8,128)(2,1)} fusion(bf16[1024,1152]{1,0:T(8,128)(2,1)} %bitcast.16, bf16[2048,1152]{1,0:T(8,128)(2,1)} %param.9), kind=kOutput, calls=%fused_computation.7 | convolution fusion | flops 4833935360 | bytes 11272192 | tf_op jit(solution)/shard_map/dot_general | solution.py:45
  152.0 0.0 reduce-scatter.3.cloned.1.call-update
  152.0 0.6 copy-done.4
  152.7 0.1 eq.8
  152.7 0.1 copy.28
  152.8 0.0 copy-done.5
  152.8 0.1 broadcast_in_dim.66
  152.9 0.1 copy.31
  153.0 4.1 %all-gather.4.cloned.1.call-done = bf16[256,4608]{1,0:T(8,128)(2,1)} async-done(((bf16[32,4608]{1,0:T(8,128)(2,1)}), bf16[256,4608]{1,0:T(8,128)(2,1)}) %all-gather.4.cloned.1.call-update) | async-done | bytes 2359312 | tf_op jit(solution)/shard_map/all_gather | solution.py:55
  157.2 37.6 %reduce-scatter.3.cloned.1.call-done = bf16[256,2048]{1,0:T(8,128)(2,1)} async-done(((bf16[1024,2048]{1,0:T(8,128)(2,1)}), bf16[256,2048]{1,0:T(8,128)(2,1)}) %reduce-scatter.3.cloned.1.call-update) | async-done | bytes 1048592 | tf_op jit(solution)/shard_map/reduce_scatter | solution.py:44
  194.7 1.9 tanh_multiply_fusion
  196.7 2.3 %gather_fusion = f32[256]{0:T(256)S(1)} fusion(f32[256,2048]{1,0:T(8,128)S(1)} %get-tuple-element.10, s32[256]{0:T(256)S(1)} %fusion.8), kind=kCustom, calls=%fused_computation | custom fusion | bytes 4096 | tf_op jit(solution)/shard_map/gather | solution.py:63
  199.0 21.5 %all-reduce = (f32[256]{0:T(256)S(1)}, f32[256]{0:T(256)S(1)}) all-reduce(f32[256]{0:T(256)S(1)} %get-tuple-element.11, f32[256]{0:T(256)S(1)} %and_select_fusion.1), channel_id=1, replica_groups=mesh['vocab'=8,'rows'=4] {'vocab'}, use_global_device_ids=true, to_apply=%region_3.4 | all-reduce | flops 512 | bytes 4096 | tf_op jit(solution)/shard_map/psum | solution.py:64
  220.5 0.1 broadcast_in_dim.63
  220.6 0.1 copy.29
  220.7 0.1 copy.30
  220.8 0.1 reshape.106
  220.9 0.1 copy.32
  221.0 0.1 reshape.107
  221.1 0.6 power_multiply_fusion
  221.7 0.0 copy-done
  221.7 1.7 broadcast_subtract_fusion
  223.3 1.4 copy.39
  (22 shorter events, 0.2 us)
Async XLA Ops:
  8.0 88.3 %reduce-scatter.5.cloned.1.call-start = ((), (), s32[]{:S(2)}) async-start(), calls=%async_computation.5 | async-start | bytes 2654208 | tf_op jit(solution)/shard_map/reduce_scatter | solution.py:36
  28.2 78.8 %copy-start.2 = (bf16[4608]{0:T(1024)(128)(2,1)S(1)}, bf16[4608]{0:T(1024)(128)(2,1)}, u32[]{:S(2)}) copy-start(bf16[4608]{0:T(1024)(128)(2,1)} %param.8) | copy-start | bytes 27652
  96.3 9.8 %all-to-all-start.1 = ((bf16[4,32,1152]{2,1,0:T(8,128)(2,1)}), bf16[4,32,1152]{2,1,0:T(8,128)(2,1)S(1)}, u32[]{:S(2)}, u32[]{:S(2)}) async-start(bf16[4,32,1152]{2,1,0:T(8,128)(2,1)} %bitcast.18), calls=%async_computation.3 | async-start | bytes 589824 | tf_op jit(solution)/shard_map/all_to_all | solution.py:53
  99.8 57.4 %all-gather.4.cloned.1.call-start = ((), (), s32[]{:S(2)}) async-start(), calls=%async_computation.6 | async-start | bytes 2654208 | tf_op jit(solution)/shard_map/all_gather | solution.py:55
  106.9 87.8 %reduce-scatter.3.cloned.1.call-start = ((), (), s32[]{:S(2)}) async-start(), calls=%async_computation.4 | async-start | bytes 5242880 | tf_op jit(solution)/shard_map/reduce_scatter | solution.py:44
  152.0 0.7 copy-start.4
  152.0 0.8 copy-start.5
  152.0 1.0 copy-start.3
  152.7 68.4 %copy-start.6 = (s32[256]{0:T(256)S(1)}, s32[256]{0:T(256)}, u32[]{:S(2)}) copy-start(s32[256]{0:T(256)} %param.13) | copy-start | bytes 3076
  194.7 26.9 %copy-start = (bf16[256,2048]{1,0:T(8,128)(2,1)S(1)}, bf16[256,2048]{1,0:T(8,128)(2,1)}, u32[]{:S(2)}) copy-start(bf16[256,2048]{1,0:T(8,128)(2,1)} %reduce-scatter.3.cloned.1.call-done) | copy-start | bytes 3145732
  199.0 24.3 %copy-start.1 = (bf16[256,4608]{1,0:T(8,128)(2,1)S(1)}, bf16[256,4608]{1,0:T(8,128)(2,1)}, u32[]{:S(2)}) copy-start(bf16[256,4608]{1,0:T(8,128)(2,1)} %all-gather.4.cloned.1.call-done) | copy-start | bytes 7077892
Sparse Core Ops, SparseCore 0:
  25.5 70.7 reduce-scatter.4
  107.1 50.0 all-gather.3
Sparse Core Ops, SparseCore 1:
  152.1 42.6 reduce-scatter.2

commit v2 on v1

--- a/solution.py
+++ b/solution.py
@@ -1,8 +1,11 @@
+import functools
 import math
 
 import jax
 import jax.numpy as jnp
 from jax import lax
+from jax.experimental import pallas as pl
+from jax.experimental.pallas import tpu as pltpu
 from jax.sharding import PartitionSpec as P
 
 BEAMS = 8
@@ -19,7 +22,7 @@
     return jnp.sum(jnp.where(hit, groups, 0.0), axis=2).reshape(-1)
 
 
-def local(shards, hidden, norm_gain, embed_table, tokens, parents, prev_scores, lengths):
+def plain(shards, hidden, norm_gain, embed_table, tokens, parents, prev_scores, lengths):
     shard_index = lax.axis_index("vocab")
     voc_rows = embed_table.shape[0]
     row_count, width = hidden.shape
@@ -70,11 +73,455 @@
     return (log_probs, chosen_lp, normalized, next_embed)
 
 
+LINE = 4
+QUARTERS = 4
+TILES = 4
+DEPTH = 512
+
+
+def kernel(
+    hidden_ref, gain_ref, table_ref, aux_ref, cap_out, stat_out, emb_out,
+    hid, table, nrm, far, aux_in, tok_t, tok_p, acc, picked, from_left, from_right, from_x,
+    quarters, emb, own, part_near, part_far, part_y, got_near, got_far, got_y, cap,
+    sum_e, sum_c, stat_in, load_sem, out_sem, send_sem, recv_sem,
+):
+    v, r = lax.axis_index("vocab"), lax.axis_index("rows")
+    z, x, y, c = v // 2, v % 2, r // 2, r % 2
+    shards = 2 * LINE
+    other_x = z * 2 + (1 - x)
+    sib = y * 2 + (1 - c)
+    far_same = (1 - y) * 2 + c
+    far_sib = (1 - y) * 2 + (1 - c)
+    voc_rows, depth = table.shape
+    rows = hid.shape[0]
+    piece = rows // shards
+    width = voc_rows // TILES
+
+    sites = []
+
+    class Site:
+        def __init__(self, cond, src, dst, device):
+            k = len(sites)
+            sites.append(self)
+            self.cond = cond
+            self.copy = pltpu.make_async_remote_copy(
+                src_ref=src, dst_ref=dst, send_sem=send_sem.at[k], recv_sem=recv_sem.at[k],
+                device_id=device, device_id_type=pl.DeviceIdType.MESH,
+            )
+
+        def start(self):
+            self.when(self.cond, self.copy.start)
+
+        def sent(self):
+            self.when(self.cond, self.copy.wait_send)
+
+        def arrived(self):
+            self.copy.wait_recv()
+
+        @staticmethod
+        def when(cond, action):
+            if cond is None:
+                action()
+            else:
+                pl.when(cond)(action)
+
+    def both(*conds):
+        return functools.reduce(jnp.logical_and, conds)
+
+    load_hidden = pltpu.make_async_copy(hidden_ref, hid, load_sem.at[0])
+    load_table = pltpu.make_async_copy(table_ref, table, load_sem.at[1])
+    load_hidden.start()
+    load_table.start()
+
+    barrier = pltpu.get_barrier_semaphore()
+    for step in range(1, QUARTERS):
+        pl.semaphore_signal(barrier, inc=1, device_id=(v, (r + step) % QUARTERS),
+                            device_id_type=pl.DeviceIdType.MESH)
+    for step in range(1, shards):
+        pl.semaphore_signal(barrier, inc=1, device_id=((v + step) % shards, r),
+                            device_id_type=pl.DeviceIdType.MESH)
+    pl.semaphore_wait(barrier, QUARTERS + shards - 2)
+
+    aux_sites = [Site(None, aux_ref, aux_in.at[s], (v, (r + s) % QUARTERS)) for s in range(1, QUARTERS)]
+    for site in aux_sites:
+        site.start()
+
+    load_hidden.wait()
+    gain = gain_ref[...].astype(jnp.float32)
+
+    def norm_step(i, _):
+        at = pl.ds(pl.multiple_of(i * 16, 16), 16)
+        states = hid[at, :].astype(jnp.float32)
+        meansq = jnp.mean(states * states, axis=-1, keepdims=True)
+        normed = (states * lax.rsqrt(meansq + norm_eps) * gain).astype(jnp.bfloat16)
+        for q in range(QUARTERS):
+            nrm[q, at, :] = normed[:, q * depth:(q + 1) * depth]
+        return 0
+
+    lax.fori_loop(0, rows // 16, norm_step, 0)
+    hid_far_sib = Site(None, nrm.at[far_sib], far.at[0], (v, far_sib))
+    hid_far_same = Site(None, nrm.at[far_same], far.at[1], (v, far_same))
+    hid_sib = Site(None, nrm.at[sib], far.at[2], (v, sib))
+    hid_sib.start()
+    hid_far_sib.start()
+    hid_far_same.start()
+
+    def columns(block):
+        return jnp.concatenate([block] * (128 // 8), axis=0).T
+
+    tok_t[r] = columns(aux_ref[...])
+    for s, site in enumerate(aux_sites, 1):
+        site.arrived()
+        tok_t[(r + QUARTERS - s) % QUARTERS] = columns(aux_in[s])
+    for p in range(shards):
+        for q in range(QUARTERS):
+            tok_p[p // 2, p % 2, q] = tok_t[q, p * piece:(p + 1) * piece, :]
+    load_table.wait()
+
+    base = (v * voc_rows).astype(jnp.float32)
+    group = QUARTERS * piece
+
+    def lookup(za, xa, zb, xb):
+        tok = jnp.concatenate(
+            [tok_p[za, xa].reshape(group, 128), tok_p[zb, xb].reshape(group, 128)], axis=0
+        )[:, :1] - base
+
+        def step(k, _):
+            entry = lax.broadcasted_iota(jnp.int32, (2 * group, DEPTH), 1) + k * DEPTH
+            hot = jnp.where(entry.astype(jnp.float32) == tok, 1.0, 0.0).astype(jnp.bfloat16)
+            at = pl.ds(pl.multiple_of(k * DEPTH, DEPTH), DEPTH)
+            acc[...] += jnp.dot(hot, table[at, :], preferred_element_type=jnp.float32)
+            return 0
+
+        acc[...] = jnp.zeros_like(acc)
+        lax.fori_loop(0, voc_rows // DEPTH, step, 0)
+        for half, (zz, xx) in enumerate(((za, xa), (zb, xb))):
+            block = acc[half * group:(half + 1) * group, :].astype(jnp.bfloat16)
+            picked[zz, xx] = block.reshape(QUARTERS, piece, depth)
+
+    even, odd = c == 0, c == 1
+    right, left = (z + 1) * 2 + x, (z - 1) * 2 + x
+
+    def line_sites(kind, view):
+        to_right, to_left = {}, {}
+        for j in range(LINE):
+            if j > 0:
+                to_right[j] = Site(both(kind, z < j), view(picked, j), view(from_left, j), (right, r))
+            if j < LINE - 1:
+                to_left[j] = Site(both(kind, z > j), view(picked, j), view(from_right, j), (left, r))
+        return to_right, to_left
+
+    even_right, even_left = line_sites(even, lambda ref, j: ref.at[j, x])
+    odd_right, odd_left = line_sites(odd, lambda ref, j: ref.at[j])
+    even_x = [Site(even, picked.at[j, 1 - x], from_x.at[j], (other_x, r)) for j in range(LINE)]
+    odd_x = Site(odd, picked.at[z, 1 - x], from_x.at[0], (other_x, r))
+
+    def add(dst, src):
+        def one(i, _):
+            dst[i] = dst[i] + src[i]
+            return 0
+
+        lax.fori_loop(0, QUARTERS, one, 0)
+
+    def line_step(kind, sites_right, sites_left, s, view):
+        j = LINE - 1 - s
+        site = sites_right[j]
+
+        def pass_right():
+            site.arrived()
+            for dst, got in view(j, from_left):
+                add(dst, got)
+
+        pl.when(both(kind, z > 0, z <= j))(pass_right)
+        other = sites_left[s]
+
+        def pass_left():
+            other.arrived()
+            for dst, got in view(s, from_right):
+                add(dst, got)
+
+        def send_right():
+            pl.when(both(kind, z > 0))(site.start)
+
+        def send_left():
+            pl.when(both(kind, z < LINE - 1))(other.start)
+
+        send_right()
+        pl.when(both(kind, z < LINE - 1, z >= s))(pass_left)
+        send_left()
+
+    even_view = lambda j, ref: [(picked.at[j, x], ref.at[j, x])]
+    odd_view = lambda j, ref: [(picked.at[j, xx], ref.at[j, xx]) for xx in range(2)]
+
+    order = (LINE - 1, 0, LINE - 2, 1)
+    for i, o in enumerate(order):
+        first = 2 * (i % 2)
+        xe = (1 - x) if i < 2 else x
+        lookup((1 - c) * first + c * o, (1 - c) * xe, (1 - c) * (first + 1) + c * o, (1 - c) * xe + c)
+        if i < 2:
+            even_x[first].start()
+            even_x[first + 1].start()
+        if o > 0:
+            pl.when(z == 0)(odd_right[o].start)
+        if o < LINE - 1:
+            pl.when(z == LINE - 1)(odd_left[o].start)
+
+    def product(block, t):
+        at = pl.ds(pl.multiple_of(t * width, width), width)
+        return lax.dot_general(block, table[at, :], (((1,), (1,)), ((), ())),
+                               preferred_element_type=jnp.float32)
+
+    near_sites = [Site(None, part_near.at[t], got_near.at[t], (v, sib)) for t in range(TILES)]
+    far_sites = [Site(None, part_far.at[t], got_far.at[t], (v, sib)) for t in range(TILES)]
+    y_sites = [Site(None, part_y.at[t], got_y.at[t], (v, far_same)) for t in range(TILES)]
+
+    hid_sib.arrived()
+    for t in range(TILES):
+        part_near[t] = product(far[2], t).astype(jnp.bfloat16)
+        near_sites[t].start()
+
+    def own_step(t, _):
+        own[t] = product(nrm[r], t)
+        return 0
+
+    lax.fori_loop(0, TILES, own_step, 0)
+
+    for s in range(LINE - 1):
+        line_step(odd, odd_right, odd_left, s, odd_view)
+
+    def odd_last():
+        odd_x.copy.start()
+
+    pl.when(odd)(odd_last)
+    for j in range(LINE):
+        def take(j=j):
+            even_x[j].arrived()
+            add(picked.at[j, x], from_x.at[j])
+
+        pl.when(even)(take)
+    for j in range(1, LINE):
+        pl.when(both(even, z == 0))(even_right[LINE - j].copy.start)
+        pl.when(both(even, z == LINE - 1))(even_left[j - 1].copy.start)
+    line_step(even, even_right, even_left, 0, even_view)
+
+    hid_far_sib.arrived()
+    for t in range(TILES):
+        part_far[t] = product(far[0], t).astype(jnp.bfloat16)
+        far_sites[t].start()
+    hid_far_same.arrived()
+    for t in range(TILES):
+        mine = product(far[1], t)
+        far_sites[t].arrived()
+        part_y[t] = (mine + got_far[t].astype(jnp.float32)).astype(jnp.bfloat16)
+        y_sites[t].start()
+
+    for s in range(1, LINE - 1):
+        line_step(even, even_right, even_left, s, even_view)
+
+    def odd_take():
+        odd_x.arrived()
+        add(picked.at[z, x], from_x.at[0])
+
+    pl.when(odd)(odd_take)
+
+    quarter_sites = [
+        Site(None, picked.at[z, x, (r + s) % QUARTERS], quarters.at[s], (v, (r + s) % QUARTERS))
+        for s in range(1, QUARTERS)
+    ]
+    for site in quarter_sites:
+        site.start()
+    whole = emb.at[z, x]
+
+    def place(q, block):
+        for k in range(QUARTERS):
+            @pl.when(q == k)
+            def _(k=k):
+                whole[:, k * depth:(k + 1) * depth] = block
+
+    place(r, picked[z, x, r])
+    for s, site in enumerate(quarter_sites, 1):
+        site.arrived()
+        place((r + QUARTERS - s) % QUARTERS, quarters[s])
+
+    go_right, go_left, go_x = {}, {}, {}
+    for j in range(LINE):
+        for xx in range(2):
+            mine = jnp.logical_or(odd, x == xx)
+            src = emb.at[j, xx]
+            go_right[j, xx] = Site(both(mine, z >= j, z < LINE - 1), src, src, (right, r))
+            go_left[j, xx] = Site(both(mine, z <= j, z > 0), src, src, (left, r))
+            go_x[j, xx] = Site(both(x == xx, jnp.logical_or(even, z == j)), src, src, (other_x, r))
+
+    def each(j, cond, action):
+        for xx in range(2):
+            pl.when(both(cond, z == j, xx == x))(functools.partial(action, j, xx))
+
+    for j in range(LINE):
+        for xx in range(2):
+            here = both(z == j, x == xx)
+            for group_of in (go_right, go_left, go_x):
+                site = group_of[j, xx]
+                pl.when(both(here, site.cond))(site.copy.start)
+    for j in range(LINE):
+        for xx in range(2):
+            there = both(odd, z == j, x == 1 - xx)
+
+            def from_neighbour(j=j, xx=xx):
+                go_x[j, xx].arrived()
+
+            pl.when(there)(from_neighbour)
+            for group_of in (go_right, go_left):
+                site = group_of[j, xx]
+                pl.when(both(there, site.cond))(site.copy.start)
+
+    def gather_step(d):
+        for j in range(LINE):
+            for xx in range(2):
+                mine = jnp.logical_or(odd, x == xx)
+                if j + d < LINE:
+                    at = both(mine, z == j + d)
+                    pl.when(at)(go_right[j, xx].arrived)
+                    pl.when(both(at, go_right[j, xx].cond))(go_right[j, xx].copy.start)
+                    pl.when(both(at, go_x[j, xx].cond))(go_x[j, xx].copy.start)
+                if j - d >= 0:
+                    at = both(mine, z == j - d)
+                    pl.when(at)(go_left[j, xx].arrived)
+                    pl.when(both(at, go_left[j, xx].cond))(go_left[j, xx].copy.start)
+                    pl.when(both(at, go_x[j, xx].cond))(go_x[j, xx].copy.start)
+
+    gather_step(1)
+    gather_step(2)
+
+    sum_e[...] = jnp.zeros_like(sum_e)
+    sum_c[...] = jnp.zeros_like(sum_c)
+    some = 32
+    out_copies = []
+    for t in range(TILES):
+        near_sites[t].arrived()
+        y_sites[t].arrived()
+
+        def cap_step(i, _, t=t):
+            at = pl.ds(pl.multiple_of(i * some, some), some)
+            logits = own[t, at, :] + got_near[t, at, :].astype(jnp.float32)
+            logits = logits + got_y[t, at, :].astype(jnp.float32)
+            capped = soft_cap * jnp.tanh(logits / soft_cap)
+            cap[at, t * width:(t + 1) * width] = capped
+            exps = jnp.exp(capped)
+            about = tok_t[r, at, :]
+            parent = about[:, 1:2].reshape(some // BEAMS, BEAMS, 1)
+            beams = capped.reshape(some // BEAMS, BEAMS, width)
+            chosen = jnp.zeros_like(beams)
+            for b in range(BEAMS):
+                chosen = jnp.where(parent == float(b), beams[:, b:b + 1, :], chosen)
+            entry = lax.broadcasted_iota(jnp.int32, (some, width), 1) + t * width
+            hit = entry.astype(jnp.float32) == about[:, 0:1] - base
+            chosen = jnp.where(hit, chosen.reshape(some, width), 0.0)
+            for k in range(0, width, 128):
+                sum_e[at, :] += exps[:, k:k + 128]
+                sum_c[at, :] += chosen[:, k:k + 128]
+            return 0
+
+        lax.fori_loop(0, rows // some, cap_step, 0)
+        span = pl.ds(t * width, width)
+        copy = pltpu.make_async_copy(cap.at[:, span], cap_out.at[:, span], out_sem.at[t])
+        copy.start()
+        out_copies.append(copy)
+    lane = lax.broadcasted_iota(jnp.int32, (rows, 128), 1)
+    total_e = jnp.sum(sum_e[...], axis=1, keepdims=True)
+    total_c = jnp.sum(sum_c[...], axis=1, keepdims=True)
+    stat = jnp.where(lane == 0, total_e, jnp.where(lane == 1, total_c, 0.0)).T[:8]
+    stat_in[0] = stat
+    stat_sites = [Site(None, stat_in.at[0], stat_in.at[s], ((v + s) % shards, r)) for s in range(1, shards)]
+    for site in stat_sites:
+        site.start()
+
+    gather_step(3)
+    for j in range(LINE):
+        for xx in range(2):
+            pl.when(both(even, x == 1 - xx))(go_x[j, xx].arrived)
+    emb_copy = pltpu.make_async_copy(emb, emb_out, out_sem.at[TILES])
+    emb_copy.start()
+    for s, site in enumerate(stat_sites, 1):
+        site.arrived()
+        stat = stat + stat_in[s]
+    stat_out[...] = stat
+    for site in sites:
+        site.sent()
+    for copy in out_copies:
+        copy.wait()
+    emb_copy.wait()
+
+
+def fused(hidden, norm_gain, embed_table, tokens, parents, prev_scores, lengths):
+    shards = 2 * LINE
+    voc_rows, depth = embed_table.shape
+    rows, features = hidden.shape
+    piece = rows // shards
+    width = voc_rows // TILES
+    aux = jnp.zeros((8, rows), jnp.float32).at[0].set(tokens.astype(jnp.float32))
+    aux = aux.at[1].set(parents.astype(jnp.float32))
+    half, full = jnp.bfloat16, jnp.float32
+    anywhere, vmem = pl.BlockSpec(memory_space=pl.ANY), pl.BlockSpec(memory_space=pltpu.VMEM)
+    tiles = pltpu.VMEM((TILES, rows, width), half)
+    line = pltpu.VMEM((LINE, 2, QUARTERS, piece, depth), half)
+    capped, stat, raw = pl.pallas_call(
+        kernel,
+        out_shape=(
+            jax.ShapeDtypeStruct((rows, voc_rows), full),
+            jax.ShapeDtypeStruct((8, rows), full),
+            jax.ShapeDtypeStruct((LINE, 2, piece, features), half),
+        ),
+        in_specs=[anywhere, vmem, anywhere, vmem],
+        out_specs=(anywhere, vmem, anywhere),
+        scratch_shapes=[
+            pltpu.VMEM((rows, features), half),
+            pltpu.VMEM((voc_rows, depth), half),
+            pltpu.VMEM((QUARTERS, rows, depth), half),
+            pltpu.VMEM((3, rows, depth), half),
+            pltpu.VMEM((QUARTERS, 8, rows), full),
+            pltpu.VMEM((QUARTERS, rows, 128), full),
+            pltpu.VMEM((LINE, 2, QUARTERS, piece, 128), full),
+            pltpu.VMEM((2 * QUARTERS * piece, depth), full),
+            line,
+            line,
+            line,
+            pltpu.VMEM((LINE, QUARTERS, piece, depth), half),
+            pltpu.VMEM((QUARTERS, piece, depth), half),
+            pltpu.VMEM((LINE, 2, piece, features), half),
+            pltpu.VMEM((TILES, rows, width), full),
+            tiles, tiles, tiles, tiles, tiles, tiles,
+            pltpu.VMEM((rows, voc_rows), full),
+            pltpu.VMEM((rows, 128), full),
+            pltpu.VMEM((rows, 128), full),
+            pltpu.VMEM((shards, 8, rows), full),
+            pltpu.SemaphoreType.DMA((2,)),
+            pltpu.SemaphoreType.DMA((TILES + 1,)),
+            pltpu.SemaphoreType.DMA((80,)),
+            pltpu.SemaphoreType.DMA((80,)),
+        ],
+        compiler_params=pltpu.CompilerParams(
+            collective_id=0, has_side_effects=True, vmem_limit_bytes=58 * 2**20
+        ),
+        cost_estimate=pl.CostEstimate(
+            flops=8 * rows * QUARTERS // 2 * voc_rows * depth, bytes_accessed=12 * 2**20,
+            transcendentals=2 * rows * voc_rows,
+        ),
+    )(hidden, norm_gain.reshape(1, features), embed_table, aux)
+    lse = jnp.log(stat[0])
+    log_probs = capped - lse[:, None]
+    chosen_lp = stat[1] - by_parent(lse, parents)
+    penalty = jnp.power((5.0 + lengths.astype(full)) / 6.0, length_power)
+    normalized = (by_parent(prev_scores, parents) + chosen_lp) / penalty
+    next_embed = (raw.reshape(rows, features).astype(full) * math.sqrt(features)).astype(half)
+    return (log_probs, chosen_lp, normalized, next_embed)
+
+
 def solution(mesh):
     placed = (P("rows", None), P(), P("vocab", "rows"), P("rows"), P("rows"), P("rows"), P("rows"))
     shards = mesh.shape["vocab"]
+    fits = shards == 2 * LINE and mesh.shape["rows"] == QUARTERS
     return jax.shard_map(
-        lambda *args: local(shards, *args),
+        fused if fits else functools.partial(plain, shards),
         mesh=mesh,
         in_specs=placed,
         out_specs=(P("rows", "vocab"), P("rows"), P("rows"), P("rows", None)),

time: 233 us -> 133 us (0.57)
  the two profiles are of different devices: /device:TPU:0 before, /device:TPU:1 now
where the time goes in v2:
time: 133 us; the launch traced here: 132 us
  Pallas kernels  120 us (90%)
  other arithmetic  6.89 us (5%)
  local copies, waits for them, and re-layouts  4.41 us (3%)
    pallas_call x1, Pallas kernels, fused(): pl.pallas_call(kernel, out_shape=(jax.ShapeDtypeStruct((rows, voc_rows),...  120 us
    sub x1, other arithmetic, fused(): log_probs = capped - lse[:, None]  3.11 us

profile of v2, /device:TPU:1, one launch (start us, length us, event | category | flops | bytes accessed | tf_op | source)
XLA Modules:
  0.0 132.4 jit_solution(6357165570178271194)
XLA Ops:
  0.6 0.7 convert_element_type.19
  1.3 0.7 convert_element_type.20
  2.0 0.0 copy-start.1
  2.0 0.8 broadcast_in_dim.26
  2.8 0.1 copy.14
  2.9 0.8 eq.8
  3.6 0.1 copy.11
  3.7 1.3 %reshape.92.gain_ref = bf16[1,4608]{1,0:T(2,128)(2,1)} reshape(bf16[4608]{0:T(1024)(128)(2,1)} %param.12) | data formatting | bytes 18432 | tf_op jit(solution)/shard_map/reshape | solution.py:509
  5.0 0.0 copy-done.1
  5.0 120.4 %shard_map.102 = (f32[256,2048]{1,0:T(8,128)}, f32[8,256]{1,0:T(8,128)}, bf16[4,2,32,4608]{3,2,1,0:T(8,128)(2,1)}) custom-call(bf16[256,4608]{1,0:T(8,128)(2,1)} %hidden_ref.1, bf16[1,4608]{1,0:T(2,128)(2,1)} %reshape.92.gain_ref, bf16[2048,1152]{1,0:T(8,128)(2,1)} %table_ref.1, f32[8,256]{1,0:T(8,128)} %copy-done.1), custom_call_target="tpu_custom_call" | custom-call | flops 9663676416 | bytes 12582912 | tf_op jit(solution)/shard_map/pallas_call | solution.py:467
  125.4 0.0 copy-start.2
  125.4 0.0 copy-start
  125.4 0.9 fusion.1
  126.3 3.1 %broadcast_subtract_fusion = f32[256,2048]{1,0:T(8,128)} fusion(f32[256,2048]{1,0:T(8,128)} %get-tuple-element.31, f32[256]{0:T(256)S(1)} %bitcast.6), kind=kLoop, calls=%fused_computation.1 | loop fusion | flops 524288 | bytes 4195328 | tf_op jit(solution)/shard_map/sub | solution.py:511
  129.4 0.1 log.19
  129.5 0.1 copy.12
  129.6 0.1 copy.15
  129.7 0.1 reshape.96
  129.8 0.1 copy.13
  129.9 0.1 reshape.95
  130.0 0.0 copy-done.2
  130.0 0.6 power_multiply_fusion
  130.6 0.0 copy-done
  130.6 1.8 %multiply_convert_fusion = bf16[4,2,32,4608]{3,2,1,0:T(8,128)(2,1)} fusion(bf16[4,2,32,4608]{3,2,1,0:T(8,128)(2,1)S(1)} %copy-done), kind=kLoop, calls=%fused_computation | loop fusion | flops 3538944 | bytes 4718592 | tf_op jit(solution)/shard_map/convert_element_type | solution.py:515
  (3 shorter events, 0.1 us)
Async XLA Ops:
  2.0 3.0 %copy-start.1 = (f32[8,256]{1,0:T(8,128)}, f32[8,256]{1,0:T(8,128)S(1)}, u32[]{:S(2)}) copy-start(f32[8,256]{1,0:T(8,128)S(1)} %scatter.9.aux_ref) | copy-start | bytes 24580
  125.4 4.6 %copy-start.2 = (s32[256]{0:T(256)S(1)}, s32[256]{0:T(256)}, u32[]{:S(2)}) copy-start(s32[256]{0:T(256)} %param.17) | copy-start | bytes 3076
  125.4 5.1 %copy-start = (bf16[4,2,32,4608]{3,2,1,0:T(8,128)(2,1)S(1)}, bf16[4,2,32,4608]{3,2,1,0:T(8,128)(2,1)}, u32[]{:S(2)}) copy-start(bf16[4,2,32,4608]{3,2,1,0:T(8,128)(2,1)} %get-tuple-element.33) | copy-start | bytes 7077892

commit v3 on v2

--- a/solution.py
+++ b/solution.py
@@ -147,7 +147,7 @@
         site.start()
 
     load_hidden.wait()
-    gain = gain_ref[...].astype(jnp.float32)
+    gain = gain_ref[...].astype(jnp.float32).reshape(1, QUARTERS * depth)
 
     def norm_step(i, _):
         at = pl.ds(pl.multiple_of(i * 16, 16), 16)
@@ -255,12 +255,12 @@
 
     order = (LINE - 1, 0, LINE - 2, 1)
     for i, o in enumerate(order):
-        first = 2 * (i % 2)
+        ea, eb = order[2 * (i % 2)], order[2 * (i % 2) + 1]
         xe = (1 - x) if i < 2 else x
-        lookup((1 - c) * first + c * o, (1 - c) * xe, (1 - c) * (first + 1) + c * o, (1 - c) * xe + c)
+        lookup((1 - c) * ea + c * o, (1 - c) * xe, (1 - c) * eb + c * o, (1 - c) * xe + c)
         if i < 2:
-            even_x[first].start()
-            even_x[first + 1].start()
+            even_x[ea].start()
+            even_x[eb].start()
         if o > 0:
             pl.when(z == 0)(odd_right[o].start)
         if o < LINE - 1:
@@ -275,34 +275,39 @@
     far_sites = [Site(None, part_far.at[t], got_far.at[t], (v, sib)) for t in range(TILES)]
     y_sites = [Site(None, part_y.at[t], got_y.at[t], (v, far_same)) for t in range(TILES)]
 
-    hid_sib.arrived()
-    for t in range(TILES):
-        part_near[t] = product(far[2], t).astype(jnp.bfloat16)
-        near_sites[t].start()
-
-    def own_step(t, _):
-        own[t] = product(nrm[r], t)
-        return 0
-
-    lax.fori_loop(0, TILES, own_step, 0)
-
-    for s in range(LINE - 1):
-        line_step(odd, odd_right, odd_left, s, odd_view)
-
-    def odd_last():
-        odd_x.copy.start()
-
-    pl.when(odd)(odd_last)
-    for j in range(LINE):
-        def take(j=j):
+    def near_products():
+        hid_sib.arrived()
+        for t in range(TILES):
+            part_near[t] = product(far[2], t).astype(jnp.bfloat16)
+            near_sites[t].start()
+
+        def own_step(t, _):
+            own[t] = product(nrm[r], t)
+            return 0
+
+        lax.fori_loop(0, TILES, own_step, 0)
+
+    def even_ready(j):
+        def take():
             even_x[j].arrived()
             add(picked.at[j, x], from_x.at[j])
 
         pl.when(even)(take)
-    for j in range(1, LINE):
-        pl.when(both(even, z == 0))(even_right[LINE - j].copy.start)
-        pl.when(both(even, z == LINE - 1))(even_left[j - 1].copy.start)
+        if j > 0:
+            pl.when(both(even, z == 0))(even_right[j].copy.start)
+        if j < LINE - 1:
+            pl.when(both(even, z == LINE - 1))(even_left[j].copy.start)
+
+    line_step(odd, odd_right, odd_left, 0, odd_view)
+    even_ready(order[0])
+    even_ready(order[1])
+    line_step(odd, odd_right, odd_left, 1, odd_view)
+    even_ready(order[2])
+    even_ready(order[3])
     line_step(even, even_right, even_left, 0, even_view)
+    line_step(odd, odd_right, odd_left, 2, odd_view)
+    pl.when(odd)(odd_x.copy.start)
+    line_step(even, even_right, even_left, 1, even_view)
 
     hid_far_sib.arrived()
     for t in range(TILES):
@@ -315,8 +320,7 @@
         part_y[t] = (mine + got_far[t].astype(jnp.float32)).astype(jnp.bfloat16)
         y_sites[t].start()
 
-    for s in range(1, LINE - 1):
-        line_step(even, even_right, even_left, s, even_view)
+    line_step(even, even_right, even_left, 2, even_view)
 
     def odd_take():
         odd_x.arrived()
@@ -389,18 +393,19 @@
                     pl.when(both(at, go_left[j, xx].cond))(go_left[j, xx].copy.start)
                     pl.when(both(at, go_x[j, xx].cond))(go_x[j, xx].copy.start)
 
+    near_products()
     gather_step(1)
-    gather_step(2)
 
     sum_e[...] = jnp.zeros_like(sum_e)
     sum_c[...] = jnp.zeros_like(sum_c)
     some = 32
     out_copies = []
-    for t in range(TILES):
+
+    def cap_tile(t):
         near_sites[t].arrived()
         y_sites[t].arrived()
 
-        def cap_step(i, _, t=t):
+        def cap_step(i, _):
             at = pl.ds(pl.multiple_of(i * some, some), some)
             logits = own[t, at, :] + got_near[t, at, :].astype(jnp.float32)
             logits = logits + got_y[t, at, :].astype(jnp.float32)
@@ -426,10 +431,29 @@
         copy = pltpu.make_async_copy(cap.at[:, span], cap_out.at[:, span], out_sem.at[t])
         copy.start()
         out_copies.append(copy)
+
+    cap_tile(0)
+    cap_tile(1)
+    gather_step(2)
+    cap_tile(2)
+    cap_tile(3)
     lane = lax.broadcasted_iota(jnp.int32, (rows, 128), 1)
     total_e = jnp.sum(sum_e[...], axis=1, keepdims=True)
     total_c = jnp.sum(sum_c[...], axis=1, keepdims=True)
-    stat = jnp.where(lane == 0, total_e, jnp.where(lane == 1, total_c, 0.0)).T[:8]
+    mine = tok_t[r]
+    parent = mine[:, 1:2].reshape(rows // BEAMS, BEAMS, 1)
+
+    def of_parent(column):
+        beams = column.reshape(rows // BEAMS, BEAMS, 1)
+        found = jnp.zeros_like(beams)
+        for b in range(BEAMS):
+            found = jnp.where(parent == float(b), beams[:, b:b + 1, :], found)
+        return found.reshape(rows, 1)
+
+    parent_e = of_parent(total_e)
+    parent_score = of_parent(mine[:, 2:3])
+    stat = jnp.where(lane == 0, total_e, jnp.where(lane == 1, total_c, jnp.where(lane == 2, parent_e, 0.0))).T[:8]
+    scores = jnp.where(lane == 3, parent_score, 0.0).T[:8]
     stat_in[0] = stat
     stat_sites = [Site(None, stat_in.at[0], stat_in.at[s], ((v + s) % shards, r)) for s in range(1, shards)]
     for site in stat_sites:
@@ -444,7 +468,7 @@
     for s, site in enumerate(stat_sites, 1):
         site.arrived()
         stat = stat + stat_in[s]
-    stat_out[...] = stat
+    stat_out[...] = stat + scores
     for site in sites:
         site.sent()
     for copy in out_copies:
@@ -458,8 +482,9 @@
     rows, features = hidden.shape
     piece = rows // shards
     width = voc_rows // TILES
-    aux = jnp.zeros((8, rows), jnp.float32).at[0].set(tokens.astype(jnp.float32))
-    aux = aux.at[1].set(parents.astype(jnp.float32))
+    line_of = lax.broadcasted_iota(jnp.int32, (8, rows), 0)
+    aux = jnp.where(line_of == 0, tokens.astype(jnp.float32)[None], prev_scores[None])
+    aux = jnp.where(line_of == 1, parents.astype(jnp.float32)[None], aux)
     half, full = jnp.bfloat16, jnp.float32
     anywhere, vmem = pl.BlockSpec(memory_space=pl.ANY), pl.BlockSpec(memory_space=pltpu.VMEM)
     tiles = pltpu.VMEM((TILES, rows, width), half)
@@ -506,12 +531,12 @@
             flops=8 * rows * QUARTERS // 2 * voc_rows * depth, bytes_accessed=12 * 2**20,
             transcendentals=2 * rows * voc_rows,
         ),
-    )(hidden, norm_gain.reshape(1, features), embed_table, aux)
+    )(hidden, norm_gain, embed_table, aux)
     lse = jnp.log(stat[0])
     log_probs = capped - lse[:, None]
-    chosen_lp = stat[1] - by_parent(lse, parents)
+    chosen_lp = stat[1] - jnp.log(stat[2])
     penalty = jnp.power((5.0 + lengths.astype(full)) / 6.0, length_power)
-    normalized = (by_parent(prev_scores, parents) + chosen_lp) / penalty
+    normalized = (stat[3] + chosen_lp) / penalty
     next_embed = (raw.reshape(rows, features).astype(full) * math.sqrt(features)).astype(half)
     return (log_probs, chosen_lp, normalized, next_embed)
 

time: 133 us -> 134 us (level)
  local copies, waits for them, and re-layouts: 4.41 us -> 0.02 us
  Pallas kernels: 120 us -> 124 us
  other arithmetic: 6.89 us -> 9.14 us
    pallas_call x1, Pallas kernels: 120 us -> 124 us  [fused(): pl.pallas_call(kernel, out_shape=(jax.ShapeDtypeStruct((rows, voc_rows),...]
    reshape x3 -> x0, local copies, waits for them, and re-layouts: 1.51 us -> none  [the longest x1 1.33 us: fused(): norm_gain.reshape(1, features)]
    select_n x0 -> x1, other arithmetic: none -> 1.35 us  [fused(): aux = jnp.where(line_of == 1, parents.astype(jnp.float32)[None], aux)]
where the time goes in v3:
time: 134 us
  Pallas kernels  124 us (93%)
  other arithmetic  9.14 us (7%)
    pallas_call x1, Pallas kernels, fused(): pl.pallas_call(kernel, out_shape=(jax.ShapeDtypeStruct((rows, voc_rows),...  124 us
    sub x1, other arithmetic, fused(): log_probs = capped - lse[:, None]  3.11 us

profile of v3, /device:TPU:1, one launch (start us, length us, event | category | flops | bytes accessed | tf_op | source)
XLA Modules:
  0.0 133.9 jit_solution(9597306384278572428)
XLA Ops:
  0.6 0.7 convert_element_type.20
  1.3 0.7 convert_element_type.19
  2.0 1.3 %select_select_fusion.aux_ref = f32[8,256]{1,0:T(8,128)} fusion(f32[256]{0:T(256)} %param.12, f32[256]{0:T(256)S(1)} %convert_element_type.20, f32[256]{0:T(256)S(1)} %convert_element_type.19, pred[8]{0:T(512)(128)(4,1)S(1)} %get-tuple-element.13, pred[8]{0:T(512)(128)(4,1)S(1)} %get-tuple-element.14), kind=kLoop, calls=%fused_computation.2 | loop fusion | flops 4096 | bytes 11280 | tf_op jit(solution)/shard_map/jit(_where)/select_n | solution.py:487
  3.3 124.1 %shard_map.102 = (f32[256,2048]{1,0:T(8,128)}, f32[8,256]{1,0:T(8,128)}, bf16[4,2,32,4608]{3,2,1,0:T(8,128)(2,1)}) custom-call(bf16[256,4608]{1,0:T(8,128)(2,1)} %hidden_ref.1, bf16[4608]{0:T(1024)(128)(2,1)} %gain_ref.1, bf16[2048,1152]{1,0:T(8,128)(2,1)} %table_ref.1, f32[8,256]{1,0:T(8,128)} %select_select_fusion.aux_ref), custom_call_target="tpu_custom_call" | custom-call | flops 9663676416 | bytes 12582912 | tf_op jit(solution)/shard_map/pallas_call | solution.py:492
  127.4 0.0 copy-start.2
  127.4 0.0 copy-start
  127.5 0.9 fusion
  128.4 0.0 copy-start.1
  128.4 3.1 %broadcast_subtract_fusion = f32[256,2048]{1,0:T(8,128)} fusion(f32[256,2048]{1,0:T(8,128)} %get-tuple-element.7, f32[256]{0:T(256)S(1)} %bitcast.5), kind=kLoop, calls=%fused_computation.1 | loop fusion | flops 524288 | bytes 4195328 | tf_op jit(solution)/shard_map/sub | solution.py:536
  131.5 0.0 copy-done.2
  131.5 0.6 power_multiply_fusion
  132.1 0.0 copy-done
  132.1 1.8 %multiply_convert_fusion = bf16[4,2,32,4608]{3,2,1,0:T(8,128)(2,1)} fusion(bf16[4,2,32,4608]{3,2,1,0:T(8,128)(2,1)S(1)} %copy-done), kind=kLoop, calls=%fused_computation | loop fusion | flops 3538944 | bytes 4718592 | tf_op jit(solution)/shard_map/convert_element_type | solution.py:540
  133.9 0.0 copy-done.1
  (1 shorter events, 0.0 us)
Async XLA Ops:
  127.4 4.1 %copy-start.2 = (s32[256]{0:T(256)S(1)}, s32[256]{0:T(256)}, u32[]{:S(2)}) copy-start(s32[256]{0:T(256)} %param.13) | copy-start | bytes 3076
  127.4 4.6 %copy-start = (bf16[4,2,32,4608]{3,2,1,0:T(8,128)(2,1)S(1)}, bf16[4,2,32,4608]{3,2,1,0:T(8,128)(2,1)}, u32[]{:S(2)}) copy-start(bf16[4,2,32,4608]{3,2,1,0:T(8,128)(2,1)} %get-tuple-element.9) | copy-start | bytes 7077892
  128.4 5.5 %copy-start.1 = (f32[1,256]{1,0:T(1,128)}, f32[1,256]{1,0:T(1,128)S(1)}, u32[]{:S(2)}) copy-start(f32[1,256]{1,0:T(1,128)S(1)} %get-tuple-element.11) | copy-start | bytes 3076

commit v4 on v3

--- a/solution.py
+++ b/solution.py
@@ -81,7 +81,7 @@
 
 def kernel(
     hidden_ref, gain_ref, table_ref, aux_ref, cap_out, stat_out, emb_out,
-    hid, table, nrm, far, aux_in, tok_t, tok_p, acc, picked, from_left, from_right, from_x,
+    hid, table, nrm, far, aux_in, tok_t, tok_p, acc, picked, from_z, from_x,
     quarters, emb, own, part_near, part_far, part_y, got_near, got_far, got_y, cap,
     sum_e, sum_c, stat_in, load_sem, out_sem, send_sem, recv_sem,
 ):
@@ -100,33 +100,22 @@
     sites = []
 
     class Site:
-        def __init__(self, cond, src, dst, device):
+        def __init__(self, src, dst, device):
             k = len(sites)
             sites.append(self)
-            self.cond = cond
             self.copy = pltpu.make_async_remote_copy(
                 src_ref=src, dst_ref=dst, send_sem=send_sem.at[k], recv_sem=recv_sem.at[k],
                 device_id=device, device_id_type=pl.DeviceIdType.MESH,
             )
 
         def start(self):
-            self.when(self.cond, self.copy.start)
+            self.copy.start()
 
         def sent(self):
-            self.when(self.cond, self.copy.wait_send)
+            self.copy.wait_send()
 
         def arrived(self):
             self.copy.wait_recv()
-
-        @staticmethod
-        def when(cond, action):
-            if cond is None:
-                action()
-            else:
-                pl.when(cond)(action)
-
-    def both(*conds):
-        return functools.reduce(jnp.logical_and, conds)
 
     load_hidden = pltpu.make_async_copy(hidden_ref, hid, load_sem.at[0])
     load_table = pltpu.make_async_copy(table_ref, table, load_sem.at[1])
@@ -142,7 +131,7 @@
                             device_id_type=pl.DeviceIdType.MESH)
     pl.semaphore_wait(barrier, QUARTERS + shards - 2)
 
-    aux_sites = [Site(None, aux_ref, aux_in.at[s], (v, (r + s) % QUARTERS)) for s in range(1, QUARTERS)]
+    aux_sites = [Site(aux_ref, aux_in.at[s], (v, (r + s) % QUARTERS)) for s in range(1, QUARTERS)]
     for site in aux_sites:
         site.start()
 
@@ -159,9 +148,9 @@
         return 0
 
     lax.fori_loop(0, rows // 16, norm_step, 0)
-    hid_far_sib = Site(None, nrm.at[far_sib], far.at[0], (v, far_sib))
-    hid_far_same = Site(None, nrm.at[far_same], far.at[1], (v, far_same))
-    hid_sib = Site(None, nrm.at[sib], far.at[2], (v, sib))
+    hid_far_sib = Site(nrm.at[far_sib], far.at[0], (v, far_sib))
+    hid_far_same = Site(nrm.at[far_same], far.at[1], (v, far_same))
+    hid_sib = Site(nrm.at[sib], far.at[2], (v, sib))
     hid_sib.start()
     hid_far_sib.start()
     hid_far_same.start()
@@ -199,22 +188,9 @@
             block = acc[half * group:(half + 1) * group, :].astype(jnp.bfloat16)
             picked[zz, xx] = block.reshape(QUARTERS, piece, depth)
 
-    even, odd = c == 0, c == 1
-    right, left = (z + 1) * 2 + x, (z - 1) * 2 + x
-
-    def line_sites(kind, view):
-        to_right, to_left = {}, {}
-        for j in range(LINE):
-            if j > 0:
-                to_right[j] = Site(both(kind, z < j), view(picked, j), view(from_left, j), (right, r))
-            if j < LINE - 1:
-                to_left[j] = Site(both(kind, z > j), view(picked, j), view(from_right, j), (left, r))
-        return to_right, to_left
-
-    even_right, even_left = line_sites(even, lambda ref, j: ref.at[j, x])
-    odd_right, odd_left = line_sites(odd, lambda ref, j: ref.at[j])
-    even_x = [Site(even, picked.at[j, 1 - x], from_x.at[j], (other_x, r)) for j in range(LINE)]
-    odd_x = Site(odd, picked.at[z, 1 - x], from_x.at[0], (other_x, r))
+    places = (LINE - 1 - z, (z + LINE // 2) % LINE, z + 1 - 2 * (z % 2), z)
+    across = [Site(picked.at[j, 1 - x], from_x.at[k], (other_x, r)) for k, j in enumerate(places)]
+    along = [Site(picked.at[j, x], from_z.at[k], (j * 2 + x, r)) for k, j in enumerate(places[:-1])]
 
     def add(dst, src):
         def one(i, _):
@@ -223,113 +199,58 @@
 
         lax.fori_loop(0, QUARTERS, one, 0)
 
-    def line_step(kind, sites_right, sites_left, s, view):
-        j = LINE - 1 - s
-        site = sites_right[j]
-
-        def pass_right():
-            site.arrived()
-            for dst, got in view(j, from_left):
-                add(dst, got)
-
-        pl.when(both(kind, z > 0, z <= j))(pass_right)
-        other = sites_left[s]
-
-        def pass_left():
-            other.arrived()
-            for dst, got in view(s, from_right):
-                add(dst, got)
-
-        def send_right():
-            pl.when(both(kind, z > 0))(site.start)
-
-        def send_left():
-            pl.when(both(kind, z < LINE - 1))(other.start)
-
-        send_right()
-        pl.when(both(kind, z < LINE - 1, z >= s))(pass_left)
-        send_left()
-
-    even_view = lambda j, ref: [(picked.at[j, x], ref.at[j, x])]
-    odd_view = lambda j, ref: [(picked.at[j, xx], ref.at[j, xx]) for xx in range(2)]
-
-    order = (LINE - 1, 0, LINE - 2, 1)
-    for i, o in enumerate(order):
-        ea, eb = order[2 * (i % 2)], order[2 * (i % 2) + 1]
-        xe = (1 - x) if i < 2 else x
-        lookup((1 - c) * ea + c * o, (1 - c) * xe, (1 - c) * eb + c * o, (1 - c) * xe + c)
-        if i < 2:
-            even_x[ea].start()
-            even_x[eb].start()
-        if o > 0:
-            pl.when(z == 0)(odd_right[o].start)
-        if o < LINE - 1:
-            pl.when(z == LINE - 1)(odd_left[o].start)
+    def take(k):
+        across[k].arrived()
+        add(picked.at[places[k], x], from_x.at[k])
+        if k < LINE - 1:
+            along[k].start()
+
+    for xx in (1 - x, x):
+        for k in (0, 2):
+            lookup(places[k], xx, places[k + 1], xx)
+            if xx is not x:
+                across[k].start()
+                across[k + 1].start()
 
     def product(block, t):
         at = pl.ds(pl.multiple_of(t * width, width), width)
         return lax.dot_general(block, table[at, :], (((1,), (1,)), ((), ())),
                                preferred_element_type=jnp.float32)
 
-    near_sites = [Site(None, part_near.at[t], got_near.at[t], (v, sib)) for t in range(TILES)]
-    far_sites = [Site(None, part_far.at[t], got_far.at[t], (v, sib)) for t in range(TILES)]
-    y_sites = [Site(None, part_y.at[t], got_y.at[t], (v, far_same)) for t in range(TILES)]
-
-    def near_products():
-        hid_sib.arrived()
-        for t in range(TILES):
-            part_near[t] = product(far[2], t).astype(jnp.bfloat16)
-            near_sites[t].start()
-
-        def own_step(t, _):
-            own[t] = product(nrm[r], t)
-            return 0
-
-        lax.fori_loop(0, TILES, own_step, 0)
-
-    def even_ready(j):
-        def take():
-            even_x[j].arrived()
-            add(picked.at[j, x], from_x.at[j])
-
-        pl.when(even)(take)
-        if j > 0:
-            pl.when(both(even, z == 0))(even_right[j].copy.start)
-        if j < LINE - 1:
-            pl.when(both(even, z == LINE - 1))(even_left[j].copy.start)
-
-    line_step(odd, odd_right, odd_left, 0, odd_view)
-    even_ready(order[0])
-    even_ready(order[1])
-    line_step(odd, odd_right, odd_left, 1, odd_view)
-    even_ready(order[2])
-    even_ready(order[3])
-    line_step(even, even_right, even_left, 0, even_view)
-    line_step(odd, odd_right, odd_left, 2, odd_view)
-    pl.when(odd)(odd_x.copy.start)
-    line_step(even, even_right, even_left, 1, even_view)
-
+    near_sites = [Site(part_near.at[t], got_near.at[t], (v, sib)) for t in range(TILES)]
+    far_sites = [Site(part_far.at[t], got_far.at[t], (v, sib)) for t in range(TILES)]
+    y_sites = [Site(part_y.at[t], got_y.at[t], (v, far_same)) for t in range(TILES)]
+
+    take(0)
+
+    def own_step(t, _):
+        own[t] = product(nrm[r], t)
+        return 0
+
+    lax.fori_loop(0, TILES, own_step, 0)
+    take(1)
+    hid_sib.arrived()
+    for t in range(TILES):
+        part_near[t] = product(far[2], t).astype(jnp.bfloat16)
+        near_sites[t].start()
+    take(2)
     hid_far_sib.arrived()
     for t in range(TILES):
         part_far[t] = product(far[0], t).astype(jnp.bfloat16)
         far_sites[t].start()
+    take(3)
     hid_far_same.arrived()
     for t in range(TILES):
         mine = product(far[1], t)
         far_sites[t].arrived()
         part_y[t] = (mine + got_far[t].astype(jnp.float32)).astype(jnp.bfloat16)
         y_sites[t].start()
-
-    line_step(even, even_right, even_left, 2, even_view)
-
-    def odd_take():
-        odd_x.arrived()
-        add(picked.at[z, x], from_x.at[0])
-
-    pl.when(odd)(odd_take)
+    for k, site in enumerate(along):
+        site.arrived()
+        add(picked.at[z, x], from_z.at[k])
 
     quarter_sites = [
-        Site(None, picked.at[z, x, (r + s) % QUARTERS], quarters.at[s], (v, (r + s) % QUARTERS))
+        Site(picked.at[z, x, (r + s) % QUARTERS], quarters.at[s], (v, (r + s) % QUARTERS))
         for s in range(1, QUARTERS)
     ]
     for site in quarter_sites:
@@ -347,54 +268,22 @@
         site.arrived()
         place((r + QUARTERS - s) % QUARTERS, quarters[s])
 
-    go_right, go_left, go_x = {}, {}, {}
-    for j in range(LINE):
-        for xx in range(2):
-            mine = jnp.logical_or(odd, x == xx)
-            src = emb.at[j, xx]
-            go_right[j, xx] = Site(both(mine, z >= j, z < LINE - 1), src, src, (right, r))
-            go_left[j, xx] = Site(both(mine, z <= j, z > 0), src, src, (left, r))
-            go_x[j, xx] = Site(both(x == xx, jnp.logical_or(even, z == j)), src, src, (other_x, r))
-
-    def each(j, cond, action):
-        for xx in range(2):
-            pl.when(both(cond, z == j, xx == x))(functools.partial(action, j, xx))
-
-    for j in range(LINE):
-        for xx in range(2):
-            here = both(z == j, x == xx)
-            for group_of in (go_right, go_left, go_x):
-                site = group_of[j, xx]
-                pl.when(both(here, site.cond))(site.copy.start)
-    for j in range(LINE):
-        for xx in range(2):
-            there = both(odd, z == j, x == 1 - xx)
-
-            def from_neighbour(j=j, xx=xx):
-                go_x[j, xx].arrived()
-
-            pl.when(there)(from_neighbour)
-            for group_of in (go_right, go_left):
-                site = group_of[j, xx]
-                pl.when(both(there, site.cond))(site.copy.start)
-
-    def gather_step(d):
-        for j in range(LINE):
-            for xx in range(2):
-                mine = jnp.logical_or(odd, x == xx)
-                if j + d < LINE:
-                    at = both(mine, z == j + d)
-                    pl.when(at)(go_right[j, xx].arrived)
-                    pl.when(both(at, go_right[j, xx].cond))(go_right[j, xx].copy.start)
-                    pl.when(both(at, go_x[j, xx].cond))(go_x[j, xx].copy.start)
-                if j - d >= 0:
-                    at = both(mine, z == j - d)
-                    pl.when(at)(go_left[j, xx].arrived)
-                    pl.when(both(at, go_left[j, xx].cond))(go_left[j, xx].copy.start)
-                    pl.when(both(at, go_x[j, xx].cond))(go_x[j, xx].copy.start)
-
-    near_products()
-    gather_step(1)
+    def piece_site(j, device):
+        at = emb.at[j, x]
+        return Site(at, at, (device, r))
+
+    give = [piece_site(z, j * 2 + x) for j in places[:-1]]
+    hand = [piece_site(j, other_x) for j in places]
+    for k in (0, 1, 2):
+        give[k].start()
+    hand[LINE - 1].start()
+
+    def gather_step(k):
+        give[k].arrived()
+        hand[k].start()
+
+    gather_step(2)
+    gather_step(0)
 
     sum_e[...] = jnp.zeros_like(sum_e)
     sum_c[...] = jnp.zeros_like(sum_c)
@@ -432,11 +321,8 @@
         copy.start()
         out_copies.append(copy)
 
-    cap_tile(0)
-    cap_tile(1)
-    gather_step(2)
-    cap_tile(2)
-    cap_tile(3)
+    for t in range(TILES):
+        cap_tile(t)
     lane = lax.broadcasted_iota(jnp.int32, (rows, 128), 1)
     total_e = jnp.sum(sum_e[...], axis=1, keepdims=True)
     total_c = jnp.sum(sum_c[...], axis=1, keepdims=True)
@@ -455,14 +341,13 @@
     stat = jnp.where(lane == 0, total_e, jnp.where(lane == 1, total_c, jnp.where(lane == 2, parent_e, 0.0))).T[:8]
     scores = jnp.where(lane == 3, parent_score, 0.0).T[:8]
     stat_in[0] = stat
-    stat_sites = [Site(None, stat_in.at[0], stat_in.at[s], ((v + s) % shards, r)) for s in range(1, shards)]
+    stat_sites = [Site(stat_in.at[0], stat_in.at[s], ((v + s) % shards, r)) for s in range(1, shards)]
     for site in stat_sites:
         site.start()
 
-    gather_step(3)
-    for j in range(LINE):
-        for xx in range(2):
-            pl.when(both(even, x == 1 - xx))(go_x[j, xx].arrived)
+    gather_step(1)
+    for site in hand:
+        site.arrived()
     emb_copy = pltpu.make_async_copy(emb, emb_out, out_sem.at[TILES])
     emb_copy.start()
     for s, site in enumerate(stat_sites, 1):
@@ -508,8 +393,7 @@
             pltpu.VMEM((LINE, 2, QUARTERS, piece, 128), full),
             pltpu.VMEM((2 * QUARTERS * piece, depth), full),
             line,
-            line,
-            line,
+            pltpu.VMEM((LINE - 1, QUARTERS, piece, depth), half),
             pltpu.VMEM((LINE, QUARTERS, piece, depth), half),
             pltpu.VMEM((QUARTERS, piece, depth), half),
             pltpu.VMEM((LINE, 2, piece, features), half),

time: 134 us -> 120 us (0.90)
  the two profiles are of different devices: /device:TPU:1 before, /device:TPU:8 now
where the time goes in v4:
time: 120 us
  Pallas kernels  110 us (92%)
  other arithmetic  9.14 us (8%)
    pallas_call x1, Pallas kernels, fused(): pl.pallas_call(kernel, out_shape=(jax.ShapeDtypeStruct((rows, voc_rows),...  110 us
    sub x1, other arithmetic, fused(): log_probs = capped - lse[:, None]  3.11 us

profile of v4, /device:TPU:8, one launch (start us, length us, event | category | flops | bytes accessed | tf_op | source)
XLA Modules:
  0.0 119.6 jit_solution(5422981510717190895)
XLA Ops:
  0.6 0.7 convert_element_type.20
  1.3 0.7 convert_element_type.19
  2.0 1.3 %select_select_fusion.aux_ref = f32[8,256]{1,0:T(8,128)} fusion(f32[256]{0:T(256)} %param.12, f32[256]{0:T(256)S(1)} %convert_element_type.20, f32[256]{0:T(256)S(1)} %convert_element_type.19, pred[8]{0:T(512)(128)(4,1)S(1)} %get-tuple-element.13, pred[8]{0:T(512)(128)(4,1)S(1)} %get-tuple-element.14), kind=kLoop, calls=%fused_computation.2 | loop fusion | flops 4096 | bytes 11280 | tf_op jit(solution)/shard_map/jit(_where)/select_n | solution.py:372
  3.3 109.8 %shard_map.102 = (f32[256,2048]{1,0:T(8,128)}, f32[8,256]{1,0:T(8,128)}, bf16[4,2,32,4608]{3,2,1,0:T(8,128)(2,1)}) custom-call(bf16[256,4608]{1,0:T(8,128)(2,1)} %hidden_ref.1, bf16[4608]{0:T(1024)(128)(2,1)} %gain_ref.1, bf16[2048,1152]{1,0:T(8,128)(2,1)} %table_ref.1, f32[8,256]{1,0:T(8,128)} %select_select_fusion.aux_ref), custom_call_target="tpu_custom_call" | custom-call | flops 9663676416 | bytes 12582912 | tf_op jit(solution)/shard_map/pallas_call | solution.py:377
  113.1 0.0 copy-start.2
  113.1 0.0 copy-start
  113.2 0.9 fusion
  114.1 0.0 copy-start.1
  114.1 3.1 %broadcast_subtract_fusion = f32[256,2048]{1,0:T(8,128)} fusion(f32[256,2048]{1,0:T(8,128)} %get-tuple-element.7, f32[256]{0:T(256)S(1)} %bitcast.5), kind=kLoop, calls=%fused_computation.1 | loop fusion | flops 524288 | bytes 4195328 | tf_op jit(solution)/shard_map/sub | solution.py:420
  117.2 0.0 copy-done.2
  117.2 0.6 power_multiply_fusion
  117.8 0.0 copy-done
  117.8 1.8 %multiply_convert_fusion = bf16[4,2,32,4608]{3,2,1,0:T(8,128)(2,1)} fusion(bf16[4,2,32,4608]{3,2,1,0:T(8,128)(2,1)S(1)} %copy-done), kind=kLoop, calls=%fused_computation | loop fusion | flops 3538944 | bytes 4718592 | tf_op jit(solution)/shard_map/convert_element_type | solution.py:424
  119.6 0.0 copy-done.1
  (1 shorter events, 0.0 us)
Async XLA Ops:
  113.1 4.1 %copy-start.2 = (s32[256]{0:T(256)S(1)}, s32[256]{0:T(256)}, u32[]{:S(2)}) copy-start(s32[256]{0:T(256)} %param.13) | copy-start | bytes 3076
  113.1 4.6 %copy-start = (bf16[4,2,32,4608]{3,2,1,0:T(8,128)(2,1)S(1)}, bf16[4,2,32,4608]{3,2,1,0:T(8,128)(2,1)}, u32[]{:S(2)}) copy-start(bf16[4,2,32,4608]{3,2,1,0:T(8,128)(2,1)} %get-tuple-element.9) | copy-start | bytes 7077892
  114.1 5.5 %copy-start.1 = (f32[1,256]{1,0:T(1,128)}, f32[1,256]{1,0:T(1,128)S(1)}, u32[]{:S(2)}) copy-start(f32[1,256]{1,0:T(1,128)S(1)} %get-tuple-element.11) | copy-start | bytes 3076

commit v5 on v4

--- a/solution.py
+++ b/solution.py
@@ -80,8 +80,8 @@
 
 
 def kernel(
-    hidden_ref, gain_ref, table_ref, aux_ref, cap_out, stat_out, emb_out,
-    hid, table, nrm, far, aux_in, tok_t, tok_p, acc, picked, from_z, from_x,
+    hidden_ref, gain_ref, table_ref, tokens_ref, parents_ref, scores_ref, cap_out, stat_out, emb_out,
+    hid, table, nrm, far, aux, aux_in, tok_t, tok_p, acc, picked, from_z, from_x,
     quarters, emb, own, part_near, part_far, part_y, got_near, got_far, got_y, cap,
     sum_e, sum_c, stat_in, load_sem, out_sem, send_sem, recv_sem,
 ):
@@ -117,6 +117,9 @@
         def arrived(self):
             self.copy.wait_recv()
 
+    row_of = lax.broadcasted_iota(jnp.int32, (8, rows), 0)
+    about = jnp.where(row_of == 0, tokens_ref[...].reshape(1, rows), parents_ref[...].reshape(1, rows))
+    aux[...] = jnp.where(row_of < 2, about.astype(jnp.float32), scores_ref[...].reshape(1, rows))
     load_hidden = pltpu.make_async_copy(hidden_ref, hid, load_sem.at[0])
     load_table = pltpu.make_async_copy(table_ref, table, load_sem.at[1])
     load_hidden.start()
@@ -131,7 +134,7 @@
                             device_id_type=pl.DeviceIdType.MESH)
     pl.semaphore_wait(barrier, QUARTERS + shards - 2)
 
-    aux_sites = [Site(aux_ref, aux_in.at[s], (v, (r + s) % QUARTERS)) for s in range(1, QUARTERS)]
+    aux_sites = [Site(aux, aux_in.at[s], (v, (r + s) % QUARTERS)) for s in range(1, QUARTERS)]
     for site in aux_sites:
         site.start()
 
@@ -158,7 +161,7 @@
     def columns(block):
         return jnp.concatenate([block] * (128 // 8), axis=0).T
 
-    tok_t[r] = columns(aux_ref[...])
+    tok_t[r] = columns(aux[...])
     for s, site in enumerate(aux_sites, 1):
         site.arrived()
         tok_t[(r + QUARTERS - s) % QUARTERS] = columns(aux_in[s])
@@ -238,13 +241,14 @@
     for t in range(TILES):
         part_far[t] = product(far[0], t).astype(jnp.bfloat16)
         far_sites[t].start()
-    take(3)
     hid_far_same.arrived()
     for t in range(TILES):
         mine = product(far[1], t)
         far_sites[t].arrived()
         part_y[t] = (mine + got_far[t].astype(jnp.float32)).astype(jnp.bfloat16)
-        y_sites[t].start()
+        if t < TILES // 2:
+            y_sites[t].start()
+    take(3)
     for k, site in enumerate(along):
         site.arrived()
         add(picked.at[z, x], from_z.at[k])
@@ -282,8 +286,8 @@
         give[k].arrived()
         hand[k].start()
 
-    gather_step(2)
-    gather_step(0)
+    for t in range(TILES // 2, TILES):
+        y_sites[t].start()
 
     sum_e[...] = jnp.zeros_like(sum_e)
     sum_c[...] = jnp.zeros_like(sum_c)
@@ -321,7 +325,11 @@
         copy.start()
         out_copies.append(copy)
 
-    for t in range(TILES):
+    cap_tile(0)
+    gather_step(2)
+    cap_tile(1)
+    gather_step(0)
+    for t in range(TILES // 2, TILES):
         cap_tile(t)
     lane = lax.broadcasted_iota(jnp.int32, (rows, 128), 1)
     total_e = jnp.sum(sum_e[...], axis=1, keepdims=True)
@@ -367,11 +375,9 @@
     rows, features = hidden.shape
     piece = rows // shards
     width = voc_rows // TILES
-    line_of = lax.broadcasted_iota(jnp.int32, (8, rows), 0)
-    aux = jnp.where(line_of == 0, tokens.astype(jnp.float32)[None], prev_scores[None])
-    aux = jnp.where(line_of == 1, parents.astype(jnp.float32)[None], aux)
     half, full = jnp.bfloat16, jnp.float32
     anywhere, vmem = pl.BlockSpec(memory_space=pl.ANY), pl.BlockSpec(memory_space=pltpu.VMEM)
+    stay = pl.BlockSpec(memory_space=pltpu.HBM)
     tiles = pltpu.VMEM((TILES, rows, width), half)
     line = pltpu.VMEM((LINE, 2, QUARTERS, piece, depth), half)
     capped, stat, raw = pl.pallas_call(
@@ -381,13 +387,14 @@
             jax.ShapeDtypeStruct((8, rows), full),
             jax.ShapeDtypeStruct((LINE, 2, piece, features), half),
         ),
-        in_specs=[anywhere, vmem, anywhere, vmem],
+        in_specs=[stay, vmem, stay, vmem, vmem, vmem],
         out_specs=(anywhere, vmem, anywhere),
         scratch_shapes=[
             pltpu.VMEM((rows, features), half),
             pltpu.VMEM((voc_rows, depth), half),
             pltpu.VMEM((QUARTERS, rows, depth), half),
             pltpu.VMEM((3, rows, depth), half),
+            pltpu.VMEM((8, rows), full),
             pltpu.VMEM((QUARTERS, 8, rows), full),
             pltpu.VMEM((QUARTERS, rows, 128), full),
             pltpu.VMEM((LINE, 2, QUARTERS, piece, 128), full),
@@ -409,13 +416,13 @@
             pltpu.SemaphoreType.DMA((80,)),
         ],
         compiler_params=pltpu.CompilerParams(
-            collective_id=0, has_side_effects=True, vmem_limit_bytes=58 * 2**20
+            collective_id=0, has_side_effects=True, vmem_limit_bytes=57 * 2**20
         ),
         cost_estimate=pl.CostEstimate(
             flops=8 * rows * QUARTERS // 2 * voc_rows * depth, bytes_accessed=12 * 2**20,
             transcendentals=2 * rows * voc_rows,
         ),
-    )(hidden, norm_gain, embed_table, aux)
+    )(hidden, norm_gain, embed_table, tokens, parents, prev_scores)
     lse = jnp.log(stat[0])
     log_probs = capped - lse[:, None]
     chosen_lp = stat[1] - jnp.log(stat[2])

time: 120 us -> 104 us (0.87)
  Pallas kernels: 110 us -> 96.4 us
  other arithmetic: 9.14 us -> 6.43 us
    pallas_call x1, Pallas kernels: 110 us -> 96.4 us  [fused(): pl.pallas_call(kernel, out_shape=(jax.ShapeDtypeStruct((rows, voc_rows),...]
    convert_element_type x2 -> x0, other arithmetic: 1.36 us -> none  [the longest x1 0.68 us: fused(): tokens.astype(jnp.float32)[None]]
    select_n x1 -> x0, other arithmetic: 1.35 us -> none  [fused(): aux = jnp.where(line_of == 1, parents.astype(jnp.float32)[None], aux)]
where the time goes in v5:
time: 104 us
  Pallas kernels  96.4 us (93%)
  other arithmetic  6.43 us (6%)
    pallas_call x1, Pallas kernels, fused(): pl.pallas_call(kernel, out_shape=(jax.ShapeDtypeStruct((rows, voc_rows),...  96.4 us
    sub x1, other arithmetic, fused(): log_probs = capped - lse[:, None]  3.11 us

profile of v5, /device:TPU:8, one launch (start us, length us, event | category | flops | bytes accessed | tf_op | source)
XLA Modules:
  0.0 103.5 jit_solution(7316183548269582663)
XLA Ops:
  0.6 96.4 %shard_map.102 = (f32[256,2048]{1,0:T(8,128)}, f32[8,256]{1,0:T(8,128)}, bf16[4,2,32,4608]{3,2,1,0:T(8,128)(2,1)}) custom-call(bf16[256,4608]{1,0:T(8,128)(2,1)} %hidden_ref.1, bf16[4608]{0:T(1024)(128)(2,1)} %gain_ref.1, bf16[2048,1152]{1,0:T(8,128)(2,1)} %table_ref.1, s32[256]{0:T(256)} %tokens_ref.1, s32[256]{0:T(256)} %parents_ref.1, f32[256]{0:T(256)} %scores_ref.1), custom_call_target="tpu_custom_call" | custom-call | flops 9663676416 | bytes 12582912 | tf_op jit(solution)/shard_map/pallas_call | solution.py:383
  97.0 0.0 copy-start.2
  97.1 0.0 copy-start
  97.1 0.9 fusion
  98.0 0.0 copy-start.1
  98.0 3.1 %broadcast_subtract_fusion = f32[256,2048]{1,0:T(8,128)} fusion(f32[256,2048]{1,0:T(8,128)} %get-tuple-element.7, f32[256]{0:T(256)S(1)} %bitcast.5), kind=kLoop, calls=%fused_computation.1 | loop fusion | flops 524288 | bytes 4195328 | tf_op jit(solution)/shard_map/sub | solution.py:427
  101.1 0.0 copy-done.2
  101.1 0.6 power_multiply_fusion
  101.7 0.0 copy-done
  101.7 1.8 %multiply_convert_fusion = bf16[4,2,32,4608]{3,2,1,0:T(8,128)(2,1)} fusion(bf16[4,2,32,4608]{3,2,1,0:T(8,128)(2,1)S(1)} %copy-done), kind=kLoop, calls=%fused_computation | loop fusion | flops 3538944 | bytes 4718592 | tf_op jit(solution)/shard_map/convert_element_type | solution.py:431
  103.5 0.0 copy-done.1
Async XLA Ops:
  97.0 4.1 %copy-start.2 = (s32[256]{0:T(256)S(1)}, s32[256]{0:T(256)}, u32[]{:S(2)}) copy-start(s32[256]{0:T(256)} %param.13) | copy-start | bytes 3076
  97.1 4.6 %copy-start = (bf16[4,2,32,4608]{3,2,1,0:T(8,128)(2,1)S(1)}, bf16[4,2,32,4608]{3,2,1,0:T(8,128)(2,1)}, u32[]{:S(2)}) copy-start(bf16[4,2,32,4608]{3,2,1,0:T(8,128)(2,1)} %get-tuple-element.9) | copy-start | bytes 7077892
  98.0 5.5 %copy-start.1 = (f32[1,256]{1,0:T(1,128)}, f32[1,256]{1,0:T(1,128)S(1)}, u32[]{:S(2)}) copy-start(f32[1,256]{1,0:T(1,128)S(1)} %get-tuple-element.11) | copy-start | bytes 3076

commit v6 on v5

--- a/solution.py
+++ b/solution.py
@@ -246,7 +246,7 @@
         mine = product(far[1], t)
         far_sites[t].arrived()
         part_y[t] = (mine + got_far[t].astype(jnp.float32)).astype(jnp.bfloat16)
-        if t < TILES // 2:
+        if t < 1:
             y_sites[t].start()
     take(3)
     for k, site in enumerate(along):
@@ -286,7 +286,7 @@
         give[k].arrived()
         hand[k].start()
 
-    for t in range(TILES // 2, TILES):
+    for t in range(1, TILES):
         y_sites[t].start()
 
     sum_e[...] = jnp.zeros_like(sum_e)
@@ -327,9 +327,8 @@
 
     cap_tile(0)
     gather_step(2)
-    cap_tile(1)
     gather_step(0)
-    for t in range(TILES // 2, TILES):
+    for t in range(1, TILES):
         cap_tile(t)
     lane = lax.broadcasted_iota(jnp.int32, (rows, 128), 1)
     total_e = jnp.sum(sum_e[...], axis=1, keepdims=True)

time: 104 us -> 102 us (0.981)
  Pallas kernels: 96.4 us -> 94.1 us
    pallas_call x1, Pallas kernels: 96.4 us -> 94.1 us  [fused(): pl.pallas_call(kernel, out_shape=(jax.ShapeDtypeStruct((rows, voc_rows),...]
where the time goes in v6:
time: 102 us; the launch traced here: 101 us
  Pallas kernels  94.1 us (92%)
  other arithmetic  6.43 us (6%)
    pallas_call x1, Pallas kernels, fused(): pl.pallas_call(kernel, out_shape=(jax.ShapeDtypeStruct((rows, voc_rows),...  94.1 us
    sub x1, other arithmetic, fused(): log_probs = capped - lse[:, None]  3.11 us

profile of v6, /device:TPU:8, one launch (start us, length us, event | category | flops | bytes accessed | tf_op | source)
XLA Modules:
  0.0 101.2 jit_solution(8625322505000333373)
XLA Ops:
  0.6 94.1 %shard_map.102 = (f32[256,2048]{1,0:T(8,128)}, f32[8,256]{1,0:T(8,128)}, bf16[4,2,32,4608]{3,2,1,0:T(8,128)(2,1)}) custom-call(bf16[256,4608]{1,0:T(8,128)(2,1)} %hidden_ref.1, bf16[4608]{0:T(1024)(128)(2,1)} %gain_ref.1, bf16[2048,1152]{1,0:T(8,128)(2,1)} %table_ref.1, s32[256]{0:T(256)} %tokens_ref.1, s32[256]{0:T(256)} %parents_ref.1, f32[256]{0:T(256)} %scores_ref.1), custom_call_target="tpu_custom_call" | custom-call | flops 9663676416 | bytes 12582912 | tf_op jit(solution)/shard_map/pallas_call | solution.py:382
  94.8 0.0 copy-start.2
  94.8 0.0 copy-start
  94.8 0.9 fusion
  95.7 0.0 copy-start.1
  95.7 3.1 %broadcast_subtract_fusion = f32[256,2048]{1,0:T(8,128)} fusion(f32[256,2048]{1,0:T(8,128)} %get-tuple-element.7, f32[256]{0:T(256)S(1)} %bitcast.5), kind=kLoop, calls=%fused_computation.1 | loop fusion | flops 524288 | bytes 4195328 | tf_op jit(solution)/shard_map/sub | solution.py:426
  98.8 0.0 copy-done.2
  98.8 0.6 power_multiply_fusion
  99.4 0.0 copy-done
  99.4 1.8 %multiply_convert_fusion = bf16[4,2,32,4608]{3,2,1,0:T(8,128)(2,1)} fusion(bf16[4,2,32,4608]{3,2,1,0:T(8,128)(2,1)S(1)} %copy-done), kind=kLoop, calls=%fused_computation | loop fusion | flops 3538944 | bytes 4718592 | tf_op jit(solution)/shard_map/convert_element_type | solution.py:430
  101.2 0.0 copy-done.1
Async XLA Ops:
  94.8 4.1 %copy-start.2 = (s32[256]{0:T(256)S(1)}, s32[256]{0:T(256)}, u32[]{:S(2)}) copy-start(s32[256]{0:T(256)} %param.13) | copy-start | bytes 3076
  94.8 4.6 %copy-start = (bf16[4,2,32,4608]{3,2,1,0:T(8,128)(2,1)S(1)}, bf16[4,2,32,4608]{3,2,1,0:T(8,128)(2,1)}, u32[]{:S(2)}) copy-start(bf16[4,2,32,4608]{3,2,1,0:T(8,128)(2,1)} %get-tuple-element.9) | copy-start | bytes 7077892
  95.7 5.5 %copy-start.1 = (f32[1,256]{1,0:T(1,128)}, f32[1,256]{1,0:T(1,128)S(1)}, u32[]{:S(2)}) copy-start(f32[1,256]{1,0:T(1,128)S(1)} %get-tuple-element.11) | copy-start | bytes 3076
